TPU v7x, 512 devices: a whole 4x8x8 slice. The times are simulated.
512 devices in a mesh: prow: 16 (over y, core), pcol: 32 (over x, z).
Axes of the slice: x: 4, y: 8, z: 8, core: 2. Of those that a mesh axis runs over, the one named last changes fastest.
Arguments:
- rhs: float32 [6, 16, 64, 128], P(None, 'prow'), may hold values from -6 to 6
- lower: float32 [6, 16, 3, 32, 128, 128], P(None, 'prow', None, 'pcol'), may hold values from -0.125 to 0.125
- lower_pattern: int32 [6, 16, 3, 32], P(None, 'prow', None, 'pcol'), may hold values from 0 to 1, as said below
- lower_inv: float32 [6, 16, 128, 128], P(None, 'prow')
- upper: float32 [6, 16, 3, 32, 128, 128], P(None, 'prow', None, 'pcol'), may hold values from -0.125 to 0.125
- upper_pattern: int32 [6, 16, 3, 32], P(None, 'prow', None, 'pcol'), may hold values from 0 to 1, as said below
- upper_inv: float32 [6, 16, 128, 128], P(None, 'prow')
Outputs:
- solution: float32 [6, 16, 64, 128], P(None, 'prow')
Inputs may be any that keep to these rules, and one draw needn't show every extreme that they name: `lower_pattern`: 1 only where the column block descends from the row block in the elimination tree. `upper_pattern`: 1 only where the row block descends from the column block in the elimination tree.
All inputs are finite; a program needn't handle non-finite values.
Results may differ from a plain program's by a relative error of at most 0.00014.
Values sent between devices are 32-bit elements; how exact they have to be, the bound alone decides.
A program may use at most 64 MiB of HBM per device.

v0:
```python
import jax
import jax.numpy as jnp
from jax import lax
from jax.sharding import PartitionSpec as P


def from_root(array, axis, root):
    mine = lax.axis_index(axis) == root
    return lax.psum(jnp.where(mine, array, jnp.zeros_like(array)), axis)


def sweep(right, blocks, pattern, inverse, order, prows, pcols, column_index):
    levels = right.shape[0]
    periods = blocks.shape[2]
    masked = blocks[:, 0, :, 0] * pattern[:, 0, :, 0].astype(jnp.float32)[:, :, None, None]
    slots = jnp.arange(periods, dtype=jnp.int32)
    store = jnp.zeros((periods,) + right.shape[1:], jnp.float32)
    solved = [None] * levels
    for turn, level in enumerate(order):
        current = right[level]
        if turn > 0:
            partial_value = jnp.einsum(
                "mkj,mij->ki", store, masked[level], precision=lax.Precision.HIGHEST
            )
            total = lax.psum(partial_value, "pcol")
            current = current - total
        value = jnp.einsum("kj,ij->ki", current, inverse[level, 0], precision=lax.Precision.HIGHEST)
        solved[level] = value
        if turn < levels - 1:
            offset = (column_index - level * prows) % pcols
            valid = offset < prows
            root = jnp.where(valid, offset, 0)
            arrived = from_root(value, "prow", root)
            slot = (level * prows + offset) // pcols
            chosen = jnp.logical_and(slots == slot, valid)
            store = jnp.where(chosen[:, None, None], arrived, store)
    return jnp.stack(solved)


def shards(rhs, lower, lower_pattern, lower_inv, upper, upper_pattern, upper_inv):
    prows = lax.axis_size("prow")
    pcols = lax.axis_size("pcol")
    column_index = lax.axis_index("pcol")
    levels = rhs.shape[0]
    forward = sweep(
        rhs[:, 0], lower, lower_pattern, lower_inv, list(range(levels)), prows, pcols, column_index
    )
    solution = sweep(
        forward,
        upper,
        upper_pattern,
        upper_inv,
        list(range(levels - 1, -1, -1)),
        prows,
        pcols,
        column_index,
    )
    return solution[:, None]


def solution(mesh):
    in_specs = (
        P(None, "prow", None, None),
        P(None, "prow", None, "pcol", None, None),
        P(None, "prow", None, "pcol"),
        P(None, "prow", None, None),
        P(None, "prow", None, "pcol", None, None),
        P(None, "prow", None, "pcol"),
        P(None, "prow", None, None),
    )
    out_specs = P(None, "prow", None, None)
    return jax.shard_map(shards, mesh=mesh, in_specs=in_specs, out_specs=out_specs, check_vma=False)
```

profile of v0, /device:TPU:1, one launch (start us, length us, event | category | flops | bytes accessed | tf_op | source)
XLA Modules:
  0.0 1838.4 jit_solution(7826475283681490098)
XLA Ops:
  0.6 0.6 compare_and_fusion
  1.1 0.7 convert_element_type.20
  1.8 0.7 convert_element_type.22
  2.7 1.1 broadcast_select_fusion.9
  3.8 49.0 %psum.140 = f32[64,128]{1,0:T(8,128)S(1)} all-reduce(f32[64,128]{1,0:T(8,128)S(1)} %get-tuple-element.5), channel_id=1, replica_groups=mesh['prow'=16,'pcol'=32] {'prow'}, use_global_device_ids=true, to_apply=%region_0.1 | all-reduce | flops 8192 | bytes 65536 | tf_op jit(solution)/shard_map/psum | solution.py:9
  52.8 1.5 bitcast_multiply_fusion.1
  54.7 118.7 %psum.141 = f32[64,128]{1,0:T(8,128)S(1)} all-reduce(f32[64,128]{1,0:T(8,128)S(1)} %convolution_bitcast_fusion.10), channel_id=1, replica_groups=mesh['prow'=16,'pcol'=32] {'pcol'}, use_global_device_ids=true, to_apply=%region_1.2 | all-reduce | flops 8192 | bytes 65536 | tf_op jit(solution)/shard_map/psum | solution.py:25
  173.4 0.9 broadcast_select_fusion.8
  174.3 73.3 %psum.142 = f32[64,128]{1,0:T(8,128)S(1)} all-reduce(f32[64,128]{1,0:T(8,128)S(1)} %get-tuple-element.7), channel_id=1, replica_groups=mesh['prow'=16,'pcol'=32] {'prow'}, use_global_device_ids=true, to_apply=%region_2.3 | all-reduce | flops 8192 | bytes 65536 | tf_op jit(solution)/shard_map/psum | solution.py:9
  248.0 110.5 %psum.143 = f32[64,128]{1,0:T(8,128)S(1)} all-reduce(f32[64,128]{1,0:T(8,128)S(1)} %convolution_bitcast_fusion.9), channel_id=1, replica_groups=mesh['prow'=16,'pcol'=32] {'pcol'}, use_global_device_ids=true, to_apply=%region_3.4 | all-reduce | flops 8192 | bytes 65536 | tf_op jit(solution)/shard_map/psum | solution.py:25
  358.5 0.8 broadcast_select_fusion.7
  359.3 73.1 %psum.144 = f32[64,128]{1,0:T(8,128)S(1)} all-reduce(f32[64,128]{1,0:T(8,128)S(1)} %get-tuple-element.9), channel_id=1, replica_groups=mesh['prow'=16,'pcol'=32] {'prow'}, use_global_device_ids=true, to_apply=%region_4.5 | all-reduce | flops 8192 | bytes 65536 | tf_op jit(solution)/shard_map/psum | solution.py:9
  432.9 110.4 %psum.145 = f32[64,128]{1,0:T(8,128)S(1)} all-reduce(f32[64,128]{1,0:T(8,128)S(1)} %convolution_bitcast_fusion.8), channel_id=1, replica_groups=mesh['prow'=16,'pcol'=32] {'pcol'}, use_global_device_ids=true, to_apply=%region_5.6 | all-reduce | flops 8192 | bytes 65536 | tf_op jit(solution)/shard_map/psum | solution.py:25
  543.3 0.9 broadcast_select_fusion.6
  544.1 73.6 %psum.146 = f32[64,128]{1,0:T(8,128)S(1)} all-reduce(f32[64,128]{1,0:T(8,128)} %get-tuple-element.11), channel_id=1, replica_groups=mesh['prow'=16,'pcol'=32] {'prow'}, use_global_device_ids=true, to_apply=%region_6.7 | all-reduce | flops 8192 | bytes 65536 | tf_op jit(solution)/shard_map/psum | solution.py:9
  617.7 1.7 convolution_bitcast_fusion.7
  619.4 110.3 %psum.147 = f32[64,128]{1,0:T(8,128)S(1)} all-reduce(f32[64,128]{1,0:T(8,128)} %convolution_bitcast_fusion.7), channel_id=1, replica_groups=mesh['prow'=16,'pcol'=32] {'pcol'}, use_global_device_ids=true, to_apply=%region_7.8 | all-reduce | flops 8192 | bytes 65536 | tf_op jit(solution)/shard_map/psum | solution.py:25
  729.7 0.9 broadcast_select_fusion.5
  730.6 73.6 %psum.148 = f32[64,128]{1,0:T(8,128)S(1)} all-reduce(f32[64,128]{1,0:T(8,128)} %get-tuple-element.13), channel_id=1, replica_groups=mesh['prow'=16,'pcol'=32] {'prow'}, use_global_device_ids=true, to_apply=%region_8.9 | all-reduce | flops 8192 | bytes 65536 | tf_op jit(solution)/shard_map/psum | solution.py:9
  804.2 1.7 convolution_bitcast_fusion.6
  805.9 110.3 %psum.149 = f32[64,128]{1,0:T(8,128)S(1)} all-reduce(f32[64,128]{1,0:T(8,128)} %convolution_bitcast_fusion.6), channel_id=1, replica_groups=mesh['prow'=16,'pcol'=32] {'pcol'}, use_global_device_ids=true, to_apply=%region_9.10 | all-reduce | flops 8192 | bytes 65536 | tf_op jit(solution)/shard_map/psum | solution.py:25
  916.7 73.0 %psum.150 = f32[64,128]{1,0:T(8,128)S(1)} all-reduce(f32[64,128]{1,0:T(8,128)S(1)} %get-tuple-element.15), channel_id=1, replica_groups=mesh['prow'=16,'pcol'=32] {'prow'}, use_global_device_ids=true, to_apply=%region_10.11 | all-reduce | flops 8192 | bytes 65536 | tf_op jit(solution)/shard_map/psum | solution.py:9
  990.8 110.4 %psum.151 = f32[64,128]{1,0:T(8,128)S(1)} all-reduce(f32[64,128]{1,0:T(8,128)S(1)} %convolution_bitcast_fusion.5), channel_id=1, replica_groups=mesh['prow'=16,'pcol'=32] {'pcol'}, use_global_device_ids=true, to_apply=%region_11.12 | all-reduce | flops 8192 | bytes 65536 | tf_op jit(solution)/shard_map/psum | solution.py:25
  1101.4 73.0 %psum.152 = f32[64,128]{1,0:T(8,128)S(1)} all-reduce(f32[64,128]{1,0:T(8,128)S(1)} %get-tuple-element.17), channel_id=1, replica_groups=mesh['prow'=16,'pcol'=32] {'prow'}, use_global_device_ids=true, to_apply=%region_12.13 | all-reduce | flops 8192 | bytes 65536 | tf_op jit(solution)/shard_map/psum | solution.py:9
  1174.9 110.4 %psum.153 = f32[64,128]{1,0:T(8,128)S(1)} all-reduce(f32[64,128]{1,0:T(8,128)S(1)} %convolution_bitcast_fusion.4), channel_id=1, replica_groups=mesh['prow'=16,'pcol'=32] {'pcol'}, use_global_device_ids=true, to_apply=%region_13.14 | all-reduce | flops 8192 | bytes 65536 | tf_op jit(solution)/shard_map/psum | solution.py:25
  1285.5 73.0 %psum.154 = f32[64,128]{1,0:T(8,128)S(1)} all-reduce(f32[64,128]{1,0:T(8,128)S(1)} %get-tuple-element.19), channel_id=1, replica_groups=mesh['prow'=16,'pcol'=32] {'prow'}, use_global_device_ids=true, to_apply=%region_14.15 | all-reduce | flops 8192 | bytes 65536 | tf_op jit(solution)/shard_map/psum | solution.py:9
  1358.9 110.4 %psum.155 = f32[64,128]{1,0:T(8,128)S(1)} all-reduce(f32[64,128]{1,0:T(8,128)S(1)} %convolution_bitcast_fusion.3), channel_id=1, replica_groups=mesh['prow'=16,'pcol'=32] {'pcol'}, use_global_device_ids=true, to_apply=%region_15.16 | all-reduce | flops 8192 | bytes 65536 | tf_op jit(solution)/shard_map/psum | solution.py:25
  1469.5 73.0 %psum.156 = f32[64,128]{1,0:T(8,128)S(1)} all-reduce(f32[64,128]{1,0:T(8,128)S(1)} %get-tuple-element.21), channel_id=1, replica_groups=mesh['prow'=16,'pcol'=32] {'prow'}, use_global_device_ids=true, to_apply=%region_16.17 | all-reduce | flops 8192 | bytes 65536 | tf_op jit(solution)/shard_map/psum | solution.py:9
  1543.0 110.4 %psum.157 = f32[64,128]{1,0:T(8,128)S(1)} all-reduce(f32[64,128]{1,0:T(8,128)S(1)} %convolution_bitcast_fusion.2), channel_id=1, replica_groups=mesh['prow'=16,'pcol'=32] {'pcol'}, use_global_device_ids=true, to_apply=%region_17.18 | all-reduce | flops 8192 | bytes 65536 | tf_op jit(solution)/shard_map/psum | solution.py:25
  1653.6 73.0 %psum.158 = f32[64,128]{1,0:T(8,128)S(1)} all-reduce(f32[64,128]{1,0:T(8,128)S(1)} %get-tuple-element.23), channel_id=1, replica_groups=mesh['prow'=16,'pcol'=32] {'prow'}, use_global_device_ids=true, to_apply=%region_18.19 | all-reduce | flops 8192 | bytes 65536 | tf_op jit(solution)/shard_map/psum | solution.py:9
  1727.0 110.4 %psum.159 = f32[64,128]{1,0:T(8,128)S(1)} all-reduce(f32[64,128]{1,0:T(8,128)S(1)} %convolution_bitcast_fusion.1), channel_id=1, replica_groups=mesh['prow'=16,'pcol'=32] {'pcol'}, use_global_device_ids=true, to_apply=%region_19.20 | all-reduce | flops 8192 | bytes 65536 | tf_op jit(solution)/shard_map/psum | solution.py:25
  1837.7 0.7 copy-done.11
  (51 shorter events, 6.4 us)
Async XLA Ops:
  0.0 432.5 %copy-start.10 = (pred[3]{0:T(512)(128)(4,1)}, pred[3]{0:T(512)(128)(4,1)S(1)}, u32[]{:S(2)}) copy-start(pred[3]{0:T(512)(128)(4,1)S(1)} %compare_and_fusion.4) | copy-start | bytes 13
  52.8 120.6 %copy-start.1 = (f32[6,1,128,128]{3,2,1,0:T(8,128)S(1)}, f32[6,1,128,128]{3,2,1,0:T(8,128)}, u32[]{:S(2)}) copy-start(f32[6,1,128,128]{3,2,1,0:T(8,128)} %param.10) | copy-start | bytes 1179652
  52.8 120.6 %copy-start.3 = (f32[6,1,64,128]{3,2,1,0:T(8,128)S(1)}, f32[6,1,64,128]{3,2,1,0:T(8,128)}, u32[]{:S(2)}) copy-start(f32[6,1,64,128]{3,2,1,0:T(8,128)} %param.7) | copy-start | bytes 589828
  248.0 668.5 %copy-start.2 = (f32[6,1,128,128]{3,2,1,0:T(8,128)S(1)}, f32[6,1,128,128]{3,2,1,0:T(8,128)}, u32[]{:S(2)}) copy-start(f32[6,1,128,128]{3,2,1,0:T(8,128)} %param.13) | copy-start | bytes 1179652
  359.3 630.4 %copy-start = (f32[6,1,3,1,128,128]{5,4,3,2,1,0:T(8,128)S(1)}, f32[6,1,3,1,128,128]{5,4,3,2,1,0:T(8,128)}, u32[]{:S(2)}) copy-start(f32[6,1,3,1,128,128]{5,4,3,2,1,0:T(8,128)} %param.11) | copy-start | bytes 3538948
  989.7 0.7 copy-start.9
  989.7 111.4 %copy-start.7 = (f32[64,128]{1,0:T(8,128)S(1)}, f32[64,128]{1,0:T(8,128)}, u32[]{:S(2)}) copy-start(f32[64,128]{1,0:T(8,128)} %get-tuple-element.14) | copy-start | bytes 98308
  989.8 184.7 %copy-start.8 = (pred[3]{0:T(512)(128)(4,1)S(1)}, pred[3]{0:T(512)(128)(4,1)}, u32[]{:S(2)}) copy-start(pred[3]{0:T(512)(128)(4,1)} %compare_and_fusion.1) | copy-start | bytes 13
  989.8 295.5 %copy-start.6 = (f32[64,128]{1,0:T(8,128)S(1)}, f32[64,128]{1,0:T(8,128)}, u32[]{:S(2)}) copy-start(f32[64,128]{1,0:T(8,128)} %get-tuple-element.12) | copy-start | bytes 98308
  990.4 478.9 %copy-start.5 = (f32[64,128]{1,0:T(8,128)S(1)}, f32[64,128]{1,0:T(8,128)}, u32[]{:S(2)}) copy-start(f32[64,128]{1,0:T(8,128)} %get-tuple-element.10) | copy-start | bytes 98308
  990.4 662.9 %copy-start.4 = (f32[64,128]{1,0:T(8,128)S(1)}, f32[64,128]{1,0:T(8,128)}, u32[]{:S(2)}) copy-start(f32[64,128]{1,0:T(8,128)} %get-tuple-element.8) | copy-start | bytes 98308
  1837.7 0.7 copy-start.11
where the time goes:
time: 1870 us; the launch traced here: 1840 us
  blocking collectives  1820 us (97%)
    psum x10, blocking collectives, sweep(): total = lax.psum(partial_value, 'pcol')  1110 us
    psum x10, blocking collectives, from_root(): return lax.psum(jnp.where(mine, array, jnp.zeros_like(array)), axis)  708 us

commit v1 on v0

v1 whole, which is shorter than its diff:
```python
import functools

import jax
import jax.numpy as jnp
from jax import lax
from jax.experimental import pallas as pl
from jax.experimental.pallas import tpu as pltpu
from jax.sharding import PartitionSpec as P

MESH = pl.DeviceIdType.MESH
NL = 6
NP = 16
NS = 8
F32 = jnp.float32


def mm_t(x, w):
    return lax.dot_general(
        x, w, (((1,), (1,)), ((), ())),
        precision=lax.Precision.HIGHEST, preferred_element_type=F32,
    )


def mm(a, b):
    return lax.dot_general(
        a, b, (((1,), (0,)), ((), ())),
        precision=lax.Precision.HIGHEST, preferred_element_type=F32,
    )


def width(level):
    return min(NP, 1 << level)


def kernel(
    lpat, upat, rhs_h, low_h, linv_h, upp_h, uinv_h, out,
    rhs, low, linv, upp, uinv, mf, mb, accf, accb, xf, xb, pf, pb, ca, cb, da, db, own,
    s_in, s_x, s_z, s_ca, s_cb, s_da, s_db, s_out, t_x0, t_a, t_b, t_ag, t_out,
):
    r = lax.axis_index("prow")
    c = lax.axis_index("pcol")
    par, q = c // NP, lax.rem(c, NP)
    even, odd = par == 0, par == 1
    yr, yq = r // 2, q // 2
    dy = lax.rem(yr - yq + 9, 8)
    owner = dy < 4
    slot = jnp.where(owner, dy * 2 + lax.rem(r, 2), 0)
    diag = r == q

    def same(level):
        return r // width(level) == q // width(level)

    def near(position, j):
        return lax.rem(position // 2 + j // 2 + 7, 8) * 2 + lax.rem(j, 2)

    def at(row, parity, col):
        return {"prow": row, "pcol": parity * NP + col}

    barrier = pltpu.get_barrier_semaphore()

    def tell(device):
        pl.semaphore_signal(barrier, inc=1, device_id=device, device_id_type=MESH)

    @pl.loop(0, NS)
    def _(j):
        s = near(r, j)
        tell(at(s, 1 - par, r))

        @pl.when(jnp.logical_not(jnp.logical_and(diag, s == r)))
        def _():
            tell(at(s, par, r))

        s2 = near(q, j)

        @pl.when(s2 != r)
        def _():
            tell(at(s2, par, q))

    @pl.when(owner)
    def _():
        @pl.loop(0, NP)
        def _(k):
            tell(at(q, 1 - par, k))

            @pl.when(jnp.logical_not(jnp.logical_and(diag, k == q)))
            def _():
                tell(at(q, par, k))

    loads = [
        (rhs_h, rhs), (linv_h, linv), (uinv_h, uinv),
    ]
    for m in range(3):
        loads.append((low_h.at[pl.ds(2 * m + 1, 5 - 2 * m), m], low.at[pl.ds(2 * m + 1, 5 - 2 * m), m]))
    for m in range(3):
        loads.append((upp_h.at[pl.ds(0, 2 * m + 1), m], upp.at[pl.ds(0, 2 * m + 1), m]))
    copies = [pltpu.make_async_copy(a, b, s_in.at[i]) for i, (a, b) in enumerate(loads)]
    for copy in copies:
        copy.start()

    accf[...] = jnp.zeros_like(accf)
    accb[...] = jnp.zeros_like(accb)
    for copy in copies[:6]:
        copy.wait()

    top = mm(uinv[5], linv[5])

    def fold(inv, block, bit):
        return mm(inv, block * bit.astype(F32))

    for m in range(3):
        for row in range(2 * m + 1, NL):
            mf[row, m] = fold(top if row == 5 else linv[row], low[row, m], lpat[row, m])

    @pl.when(diag)
    def _():
        for row in range(1, NL):
            @pl.when(par == (row - 1) % 2)
            def _(row=row):
                accf[row] = mm_t(rhs[row], top if row == 5 else linv[row]).reshape(NS, 8, 128)

        @pl.when(even)
        def _():
            xf[0] = mm_t(rhs[0], linv[0]).reshape(NS, 8, 128)

    to_self = jnp.where(diag, 1, 0)
    pl.semaphore_wait(barrier, jnp.where(owner, NP - 1 + 2 * NP + 2 * NS - 2 * to_self, 2 * NS))

    @pl.when(jnp.logical_and(diag, even))
    def _():
        @pl.loop(1, NP)
        def _(d):
            pltpu.make_async_remote_copy(
                xf.at[0], xf.at[0], t_x0.at[d], s_x.at[0],
                device_id=at(jnp.bitwise_xor(r, d), par, q), device_id_type=MESH,
            ).start()

    def send_slices(source, target, place, send_sem, recv_sem, parity):
        for j in range(NS):
            s = near(r, j)

            def remote(j=j, s=s):
                pltpu.make_async_remote_copy(
                    source.at[j], target.at[place], send_sem, recv_sem,
                    device_id=at(s, parity, r), device_id_type=MESH,
                ).start()

            if parity is par:
                me = jnp.logical_and(diag, s == r)
                pl.when(jnp.logical_not(me))(remote)

                @pl.when(me)
                def _(j=j):
                    pltpu.make_async_copy(source.at[j], target.at[place], recv_sem).start()
            else:
                remote()

    def wait_bytes(ref, sem):
        pltpu.make_async_copy(ref, ref, sem).wait()

    def wait_sent_slices(source, send_sem, same_parity):
        if not same_parity:
            wait_bytes(source, send_sem)
            return

        @pl.when(diag)
        def _():
            wait_bytes(source.at[pl.ds(0, NS - 1)], send_sem)

        @pl.when(jnp.logical_not(diag))
        def _():
            wait_bytes(source, send_sem)

    def wait_slices(ref, sem):
        @pl.when(owner)
        def _():
            wait_bytes(ref.at[pl.ds(0, NS - 1)], sem)

        @pl.when(jnp.logical_not(owner))
        def _():
            wait_bytes(ref, sem)

    def spread(level, store, sem, wide):
        @pl.loop(1, wide + 1 if wide < NP else NP)
        def _(d):
            if wide == NP:
                row = jnp.bitwise_xor(r, d)
            else:
                row = q // wide * wide + d - 1

            @pl.when(row != r)
            def _():
                pltpu.make_async_remote_copy(
                    own.at[level], store.at[level, slot], t_ag.at[level], sem.at[level],
                    device_id=at(row, par, q), device_id_type=MESH,
                ).start()

    def deliver(level):
        @pl.loop(0, NP)
        def _(k):
            pltpu.make_async_remote_copy(
                own.at[NL + level], out.at[level, slot], t_out.at[level], s_out,
                device_id=at(q, 1 - par, k), device_id_type=MESH,
            ).start()
            me = jnp.logical_and(diag, k == q)

            @pl.when(jnp.logical_not(me))
            def _():
                pltpu.make_async_remote_copy(
                    own.at[NL + level], out.at[level, slot], t_out.at[level], s_out,
                    device_id=at(q, par, k), device_id_type=MESH,
                ).start()

            @pl.when(me)
            def _():
                pltpu.make_async_copy(own.at[NL + level], out.at[level, slot], s_out).start()

    def forward_hold(level):
        m = level // 2
        if level == 0:
            @pl.when(jnp.logical_not(diag))
            def _():
                wait_bytes(xf.at[0], s_x.at[0])
        else:
            wait_slices(xf.at[level], s_x.at[level])
        x = xf[level].reshape(64, 128)

        @pl.when(same(level + 1))
        def _():
            pf[level] = accf[level + 1] - mm_t(x, mf[level + 1, m]).reshape(NS, 8, 128)
            send_slices(pf.at[level], ca, (level + 1) * NP + lax.rem(q, width(level + 1)), t_a.at[level + 1], s_ca.at[level + 1], 1 - par)

        for row in range(level + 2, NL):
            @pl.when(same(row))
            def _(row=row):
                accf[row] = accf[row] - mm_t(x, mf[row, m]).reshape(NS, 8, 128)
                if row == level + 2:
                    send_slices(accf.at[row], cb, row * NP + lax.rem(q, width(row)), t_b.at[row], s_cb.at[row], par)

        @pl.when(diag)
        def _():
            accb[level] = mm_t(x, uinv[level]).reshape(NS, 8, 128)
            if level == 4:
                send_slices(accb.at[4], db, 4 * NP, t_b.at[NL + 4], s_db.at[4], par)

    def forward_own(level):
        n = width(level)
        wait_bytes(ca.at[pl.ds(level * NP, n)], s_ca.at[level])
        total = jnp.sum(ca[level * NP:level * NP + n], axis=0)
        if level >= 2:
            wait_bytes(cb.at[pl.ds(level * NP, n)], s_cb.at[level])
            total = total + jnp.sum(cb[level * NP:level * NP + n], axis=0)
        if level == 5:
            own[NL + 5] = total
            own[5] = total
            xb[5, slot] = total
            spread(5, xb, s_z, NP)
            deliver(5)
        else:
            own[level] = total
            xf[level, slot] = total
            spread(level, xf, s_x, NP)

    def back_hold(level):
        m = level // 2
        row = level - 1

        @pl.when(same(level))
        def _():
            wait_slices(xb.at[level], s_z.at[level])
            z = xb[level].reshape(64, 128)
            pb[row] = accb[row] - mm_t(z, mb[row, m]).reshape(NS, 8, 128)

        @pl.when(jnp.logical_not(same(level)))
        def _():
            pb[row] = accb[row]

        send_slices(pb.at[row], da, row * NP + q, t_a.at[NL + row], s_da.at[row], 1 - par)

        if level >= 2:
            @pl.when(same(level))
            def _():
                z = xb[level].reshape(64, 128)
                for lower in range(level - 2, -1, -1):
                    accb[lower] = accb[lower] - mm_t(z, mb[lower, m]).reshape(NS, 8, 128)
            send_slices(accb.at[level - 2], db, (level - 2) * NP + q, t_b.at[NL + level - 2], s_db.at[level - 2], par)

    def back_own(level):
        wait_bytes(da.at[pl.ds(level * NP, NP)], s_da.at[level])
        total = jnp.sum(da[level * NP:level * NP + NP], axis=0)
        n = 1 if level == 4 else NP
        wait_bytes(db.at[pl.ds(level * NP, n)], s_db.at[level])
        total = total + jnp.sum(db[level * NP:level * NP + n], axis=0)
        own[NL + level] = total
        if level > 0:
            @pl.when(same(level))
            def _():
                xb[level, slot] = total
            spread_back(level)
        deliver(level)

    def spread_back(level):
        wide = width(level)

        @pl.loop(0, wide)
        def _(d):
            row = q // wide * wide + d

            @pl.when(row != r)
            def _():
                pltpu.make_async_remote_copy(
                    own.at[NL + level], xb.at[level, slot], t_ag.at[NL + level], s_z.at[level],
                    device_id=at(row, par, q), device_id_type=MESH,
                ).start()

    def prepare_back():
        for copy in copies[6:]:
            copy.wait()
        for m in range(3):
            for row in range(0, 2 * m + 1):
                mb[row, m] = fold(uinv[row], upp[row, m], upat[row, m])

    def run(parity):
        first = True
        for level in range(NL):
            if level % 2 == parity:
                if level > 0:
                    pl.when(owner)(functools.partial(forward_own, level))
                if level < 5:
                    forward_hold(level)
                if first:
                    prepare_back()
                    first = False
        for level in range(NL - 1, -1, -1):
            if level % 2 == parity:
                if level < 5:
                    pl.when(owner)(functools.partial(back_own, level))
                if level > 0:
                    back_hold(level)

    @pl.when(even)
    def _():
        run(0)

    @pl.when(odd)
    def _():
        run(1)

    @pl.when(jnp.logical_and(diag, even))
    def _():
        @pl.loop(1, NP)
        def _(d):
            wait_bytes(xf.at[0], t_x0.at[d])

    for level in range(NL):
        if level < 5:
            @pl.when(jnp.logical_and(par == level % 2, same(level + 1)))
            def _(level=level):
                wait_sent_slices(pf.at[level], t_a.at[level + 1], False)
            if level + 2 < NL:
                @pl.when(jnp.logical_and(par == level % 2, same(level + 2)))
                def _(level=level):
                    wait_sent_slices(accf.at[level + 2], t_b.at[level + 2], True)
        if level > 0:
            @pl.when(par == level % 2)
            def _(level=level):
                wait_sent_slices(pb.at[level - 1], t_a.at[NL + level - 1], False)
                if level >= 2:
                    wait_sent_slices(accb.at[level - 2], t_b.at[NL + level - 2], True)

    @pl.when(jnp.logical_and(diag, even))
    def _():
        wait_sent_slices(accb.at[4], t_b.at[NL + 4], True)

    @pl.when(owner)
    def _():
        for level in range(NL):
            @pl.when(par == level % 2)
            def _(level=level):
                if level > 0:
                    wait_bytes(da.at[pl.ds(0, NP - 1)], t_ag.at[level])
                if 0 < level < 5:
                    @pl.when(same(level))
                    def _():
                        if width(level) > 1:
                            wait_bytes(da.at[pl.ds(0, width(level) - 1)], t_ag.at[NL + level])

                    @pl.when(jnp.logical_not(same(level)))
                    def _():
                        wait_bytes(da.at[pl.ds(0, width(level))], t_ag.at[NL + level])

                @pl.when(diag)
                def _():
                    wait_bytes(da.at[pl.ds(0, 2 * NP - 1)], t_out.at[level])

                @pl.when(jnp.logical_not(diag))
                def _():
                    wait_bytes(da.at[pl.ds(0, 2 * NP)], t_out.at[level])

    wait_bytes(out, s_out)


def shards(rhs, lower, lower_pattern, lower_inv, upper, upper_pattern, upper_inv):
    v = pltpu.VMEM
    dma = pltpu.SemaphoreType.DMA
    slices = (NL, NS, 8, 128)
    parts = (NL * NP, 8, 128)
    blocks = (NL, 3, 128, 128)
    got = pl.pallas_call(
        kernel,
        out_shape=jax.ShapeDtypeStruct(slices, F32),
        in_specs=[pl.BlockSpec(memory_space=pltpu.SMEM)] * 2 + [pl.BlockSpec(memory_space=pl.ANY)] * 5,
        out_specs=pl.BlockSpec(memory_space=pltpu.VMEM),
        scratch_shapes=[
            v((NL, 64, 128), F32), v(blocks, F32), v((NL, 128, 128), F32), v(blocks, F32), v((NL, 128, 128), F32),
            v(blocks, F32), v(blocks, F32), v(slices, F32), v(slices, F32), v(slices, F32), v(slices, F32),
            v(slices, F32), v(slices, F32), v(parts, F32), v(parts, F32), v(parts, F32), v(parts, F32),
            v((2 * NL, 8, 128), F32),
            dma((9,)), dma((NL,)), dma((NL,)), dma((NL,)), dma((NL,)), dma((NL,)), dma((NL,)), dma,
            dma((NP,)), dma((2 * NL,)), dma((2 * NL,)), dma((2 * NL,)), dma((NL,)),
        ],
        compiler_params=pltpu.CompilerParams(
            collective_id=0, has_side_effects=True, vmem_limit_bytes=32 * 1024 * 1024
        ),
        name="substitution",
    )(
        lower_pattern.reshape(NL, 3), upper_pattern.reshape(NL, 3), rhs.reshape(NL, 64, 128),
        lower.reshape(blocks), lower_inv.reshape(NL, 128, 128), upper.reshape(blocks), upper_inv.reshape(NL, 128, 128),
    )
    return got.reshape(NL, 1, 64, 128)


def solution(mesh):
    in_specs = (
        P(None, "prow", None, None),
        P(None, "prow", None, "pcol", None, None),
        P(None, "prow", None, "pcol"),
        P(None, "prow", None, None),
        P(None, "prow", None, "pcol", None, None),
        P(None, "prow", None, "pcol"),
        P(None, "prow", None, None),
    )
    out_specs = P(None, "prow", None, None)
    return jax.shard_map(shards, mesh=mesh, in_specs=in_specs, out_specs=out_specs, check_vma=False)
```

time: 1870 us -> 146 us (0.08)
  the two profiles are of different devices: /device:TPU:1 before, /device:TPU:63 now
where the time goes in v1:
time: 146 us; the launch traced here: 145 us
  Pallas kernels  138 us (95%)
  local copies, waits for them, and re-layouts  7.67 us (5%)
    pallas_call x1, Pallas kernels, shards(): pl.pallas_call(kernel, out_shape=jax.ShapeDtypeStruct(slices, F32), in_sp...  138 us
    unnamed x11, local copies, waits for them, and re-layouts  6.14 us

profile of v1, /device:TPU:63, one launch (start us, length us, event | category | flops | bytes accessed | tf_op | source)
XLA Modules:
  0.0 145.5 jit_solution(4690282135412576094)
XLA Ops:
  0.0 0.8 copy.11
  0.8 0.8 copy.12
  1.5 0.0 copy-start
  1.5 1.3 copy-done
  2.8 0.0 copy-start.1
  2.8 1.3 copy-done.1
  4.1 0.0 copy-start.2
  4.1 1.0 copy-done.2
  5.1 0.0 copy-start.3
  5.1 1.0 copy-done.3
  6.1 0.0 copy-start.4
  6.1 0.9 copy-done.4
  7.0 137.8 %substitution.1 = f32[6,8,8,128]{3,2,1,0:T(8,128)S(1)} custom-call(s32[6,3]{1,0:T(8,128)S(1)} %bitcast.16, s32[6,3]{1,0:T(8,128)S(1)} %bitcast.17, f32[6,64,128]{2,1,0:T(8,128)S(1)} %bitcast.15, f32[6,3,128,128]{3,2,1,0:T(8,128)S(1)} %bitcast.10, f32[6,128,128]{2,1,0:T(8,128)S(1)} %bitcast.13, f32[6,3,128,128]{3,2,1,0:T(8,128)S(1)} %bitcast.11, ...), custom_call_target="tpu_custom_call" | custom-call | tf_op jit(solution)/shard_map/substitution/pallas_call | solution.py:408
  144.8 0.7 copy.14
Async XLA Ops:
  1.5 1.3 copy-start
  2.8 1.3 copy-start.1
  4.1 1.0 copy-start.2
  5.1 1.0 copy-start.3
  6.1 0.9 copy-start.4

commit v2 on v0

v2 whole, which is shorter than its diff:
```python
import functools

import jax
import jax.numpy as jnp
from jax import lax
from jax.experimental import pallas as pl
from jax.experimental.pallas import tpu as pltpu
from jax.sharding import PartitionSpec as P

MESH = pl.DeviceIdType.MESH
NL = 6
NP = 16
NS = 8
BF16 = jnp.bfloat16
F32 = jnp.float32


def mm_t(x, w):
    return lax.dot_general(
        x, w, (((1,), (1,)), ((), ())),
        precision=lax.Precision.HIGHEST, preferred_element_type=F32,
    )


def mm(a, b):
    return lax.dot_general(
        a, b, (((1,), (0,)), ((), ())),
        precision=lax.Precision.HIGHEST, preferred_element_type=F32,
    )


HELD = {}
for _row, _col in ((5, 4), (4, 5), (3, 4), (2, 3), (1, 3), (0, 3), (1, 2), (0, 2), (0, 1)):
    HELD[_row, _col] = (sum(n for _, n in HELD.values()), min(NP, 1 << _col))
NHELD = sum(n for _, n in HELD.values())
GROUP = {key: i for i, key in enumerate(HELD)}
GATHERED = {"x4": (0, 16), "z5": (16, 16), "z4": (32, 16), "z3": (48, 8), "z2": (56, 4), "z1": (60, 2)}
STEP = {key: i for i, key in enumerate(GATHERED)}
NGATHERED = 62


def split(x):
    high = x.astype(BF16)
    return high, (x - high.astype(F32)).astype(BF16)


def dot_t(x, w):
    return lax.dot_general(x, w, (((1,), (1,)), ((), ())), preferred_element_type=F32)


def width(level):
    return min(NP, 1 << level)


def kernel(
    lpat, upat, rhs_h, low_h, linv_h, upp_h, uinv_h, out,
    rhs, low, linv, upp, uinv, mf, mb, accf, accb, xf, xb, pf, ca, cb, own,
    held, wh, wl, seen, mine, r4, r5, r45, d3, d5, d4,
    s_in, s_x, s_z, s_ca, s_cb, s_held, s_seen, s_rows, s_out,
    t_x0, t_a, t_b, t_ag, t_held, t_seen, t_rows, t_z, t_out,
):
    r = lax.axis_index("prow")
    c = lax.axis_index("pcol")
    par, q = c // NP, lax.rem(c, NP)
    even, odd = par == 0, par == 1
    dy = lax.rem(r // 2 - q // 2 + 9, 8)
    owner = dy < 4
    slot = jnp.where(owner, dy * 2 + lax.rem(r, 2), 0)
    diag = r == q
    col_x, col_z = c // 8, lax.rem(c, 8)
    turned = lax.rem(col_z + 8 - 2 * lax.rem(col_x, 2), 8)
    team = lax.rem(turned, 4) == 0
    k_me = jnp.where(team, col_x * 2 + turned // 4, 0)

    def seat(k):
        return 8 * (k // 2) + 4 * lax.rem(k, 2) + 2 * lax.rem(k // 2, 2)

    def same(level):
        return r // width(level) == q // width(level)

    def near(position, j):
        return lax.rem(position // 2 + j // 2 + 7, 8) * 2 + lax.rem(j, 2)

    def at(row, col):
        return {"prow": row, "pcol": col}

    barrier = pltpu.get_barrier_semaphore()

    def tell(row, col):
        @pl.when(jnp.logical_not(jnp.logical_and(row == r, col == c)))
        def _():
            pl.semaphore_signal(barrier, inc=1, device_id=at(row, col), device_id_type=MESH)

    @pl.loop(0, NS)
    def _(j):
        tell(near(q, j), c)
        tell(r, seat(j))
        tell(q, seat(j))

    @pl.when(owner)
    def _():
        @pl.loop(0, 2 * NP)
        def _(k):
            tell(q, k)

    @pl.when(team)
    def _():
        @pl.loop(0, 2 * NP)
        def _(k):
            tell(r, k)

        @pl.loop(0, NP)
        def _(k):
            tell(k, c)

    loads = [(rhs_h, rhs), (linv_h, linv), (uinv_h, uinv)]
    for m in range(3):
        loads.append((low_h.at[pl.ds(2 * m + 1, 5 - 2 * m), m], low.at[pl.ds(2 * m + 1, 5 - 2 * m), m]))
    for m in range(3):
        loads.append((upp_h.at[pl.ds(0, 2 * m + 1), m], upp.at[pl.ds(0, 2 * m + 1), m]))
    copies = [pltpu.make_async_copy(a, b, s_in.at[i]) for i, (a, b) in enumerate(loads)]
    for copy in copies:
        copy.start()

    accf[...] = jnp.zeros_like(accf)
    accb[...] = jnp.zeros_like(accb)
    for copy in copies[:6]:
        copy.wait()

    top = mm(uinv[5], linv[5])

    def fold(inv, block, bit):
        return mm(inv, block * bit.astype(F32))

    for m in range(3):
        for row in range(2 * m + 1, NL):
            mf[row, m] = fold(top if row == 5 else linv[row], low[row, m], lpat[row, m])

    @pl.when(diag)
    def _():
        for row in range(1, NL):
            @pl.when(par == (row - 1) % 2)
            def _(row=row):
                accf[row] = mm_t(rhs[row], top if row == 5 else linv[row]).reshape(NS, 8, 128)

        @pl.when(even)
        def _():
            xf[0] = mm_t(rhs[0], linv[0]).reshape(NS, 8, 128)

    one = jnp.where(diag, 1, 0)
    sat = jnp.where(team, 1, 0)
    expected = 2 * NS - one + jnp.where(owner, NP - 1, 0) + NS - sat
    expected = expected + jnp.where(team, 2 * NP - 1 + NP - 1 + 2 * NP - one, 0)
    pl.semaphore_wait(barrier, expected)

    def wait_bytes(ref, sem):
        pltpu.make_async_copy(ref, ref, sem).wait()

    def push(source, target, send_sem, recv_sem, row, col, may_be_me):
        def remote():
            pltpu.make_async_remote_copy(
                source, target, send_sem, recv_sem, device_id=at(row, col), device_id_type=MESH
            ).start()

        if not may_be_me:
            remote()
            return
        me = jnp.logical_and(row == r, col == c)
        pl.when(jnp.logical_not(me))(remote)

        @pl.when(me)
        def _():
            pltpu.make_async_copy(source, target, recv_sem).start()

    @pl.when(jnp.logical_and(diag, even))
    def _():
        @pl.loop(1, NP)
        def _(d):
            push(xf.at[0], xf.at[0], t_x0.at[d], s_x.at[0], jnp.bitwise_xor(r, d), c, False)

    def to_owners(source, target, place, send_sem, recv_sem, parity):
        for j in range(NS):
            push(source.at[j], target.at[place], send_sem, recv_sem, near(r, j), parity * NP + r, parity is par)

    def to_team(piece, target, send_sem, recv_sem):
        for k in range(NS):
            push(piece(k), target, send_sem, recv_sem, r, seat(k), True)

    def wait_slices(ref, sem):
        @pl.when(owner)
        def _():
            wait_bytes(ref.at[pl.ds(0, NS - 1)], sem)

        @pl.when(jnp.logical_not(owner))
        def _():
            wait_bytes(ref, sem)

    def give(row, col, source):
        first, n = HELD[row, col]
        i = GROUP[row, col]

        @pl.when(same(col))
        def _():
            @pl.loop(0, NS)
            def _(k):
                push(source, held.at[first + lax.rem(q, n)], t_held.at[i], s_held.at[i], r, seat(k), True)

    def minus(ref, row, x, w):
        ref[row] = ref[row] - mm_t(x, w).reshape(NS, 8, 128)

    def forward_hold(level):
        m = level // 2
        if level == 0:
            @pl.when(jnp.logical_not(diag))
            def _():
                wait_bytes(xf.at[0], s_x.at[0])
        else:
            wait_slices(xf.at[level], s_x.at[level])
        x = xf[level].reshape(64, 128)
        if level < 3:
            @pl.when(same(level + 1))
            def _():
                row = level + 1
                pf[level] = accf[row] - mm_t(x, mf[row, m]).reshape(NS, 8, 128)
                to_owners(pf.at[level], ca, row * NP + lax.rem(q, width(row)), t_a.at[row], s_ca.at[row], 1 - par)

            row = level + 2
            if row < 4:
                @pl.when(same(row))
                def _():
                    minus(accf, row, x, mf[row, m])
                    to_owners(accf.at[row], cb, row * NP + lax.rem(q, width(row)), t_b.at[row], s_cb.at[row], par)

            for row in range(level + 3, 4):
                @pl.when(same(row))
                def _(row=row):
                    minus(accf, row, x, mf[row, m])

            minus(accf, 4, x, mf[4, m])
            minus(accf, 5, x, mf[5, m])
            if level == 2:
                to_team(lambda k: accf.at[pl.ds(4, 2), k], r45.at[q], t_rows.at[0], s_rows.at[0])
        else:
            minus(accf, 4, x, mf[4, m])
            to_team(lambda k: accf.at[4, k], r4.at[q], t_rows.at[1], s_rows.at[1])
            minus(accf, 5, x, mf[5, m])
            to_team(lambda k: accf.at[5, k], r5.at[q], t_rows.at[2], s_rows.at[2])

        @pl.when(diag)
        def _():
            accb[level] = mm_t(x, uinv[level]).reshape(NS, 8, 128)

    def forward_own(level):
        n = width(level)
        wait_bytes(ca.at[pl.ds(level * NP, n)], s_ca.at[level])
        total = jnp.sum(ca[level * NP:level * NP + n], axis=0)
        if level >= 2:
            wait_bytes(cb.at[pl.ds(level * NP, n)], s_cb.at[level])
            total = total + jnp.sum(cb[level * NP:level * NP + n], axis=0)
        own[level] = total
        xf[level, slot] = total

        @pl.loop(1, NP)
        def _(d):
            push(own.at[level], xf.at[level, slot], t_ag.at[level], s_x.at[level], jnp.bitwise_xor(r, d), c, False)

    def prepare_back():
        for copy in copies[6:]:
            copy.wait()
        for m in range(3):
            for row in range(0, 2 * m + 1):
                mb[row, m] = fold(uinv[row], upp[row, m], upat[row, m])

    @pl.when(even)
    def _():
        forward_hold(0)
        give(5, 4, mf.at[5, 2])
        prepare_back()
        pl.when(owner)(functools.partial(forward_own, 2))
        forward_hold(2)
        give(3, 4, mb.at[3, 2])
        give(1, 2, mb.at[1, 1])
        give(0, 2, mb.at[0, 1])

    @pl.when(odd)
    def _():
        prepare_back()
        pl.when(owner)(functools.partial(forward_own, 1))
        forward_hold(1)
        give(4, 5, mb.at[4, 2])
        pl.when(owner)(functools.partial(forward_own, 3))
        forward_hold(3)
        give(2, 3, mb.at[2, 1])
        give(1, 3, mb.at[1, 1])
        give(0, 3, mb.at[0, 1])
        give(0, 1, mb.at[0, 0])

    def take(row, col):
        first, n = HELD[row, col]
        wait_bytes(held.at[pl.ds(first, n)], s_held.at[GROUP[row, col]])
        for i in range(first // 2, (first + n) // 2):
            high, low_ = split(jnp.concatenate([held[2 * i], held[2 * i + 1]], axis=1))
            wh[i] = high
            wl[i] = low_

    def apply(row, col, name):
        first, n = HELD[row, col]
        base, _ = GATHERED[name]
        total = jnp.zeros((8, 128), F32)
        for i in range(n // 2):
            high, low_ = split(jnp.concatenate([seen[base + 2 * i], seen[base + 2 * i + 1]], axis=1))
            both = dot_t(jnp.concatenate([high, low_], axis=0), wh[first // 2 + i])
            total = total + both[0:8] + both[8:16] + dot_t(high, wl[first // 2 + i])
        return total

    def gather(name, value):
        base, n = GATHERED[name]
        i = STEP[name]
        mine[i] = value
        place = base + lax.rem(r, n)
        seen[place] = value

        @pl.loop(1, n)
        def _(d):
            push(mine.at[i], seen.at[place], t_seen.at[i], s_seen.at[i], jnp.bitwise_xor(r, d), c, False)

    def gathered(name):
        base, n = GATHERED[name]
        wait_bytes(seen.at[pl.ds(base, n - 1)], s_seen.at[STEP[name]])

    def to_holders(level, name):
        @pl.loop(0, NP)
        def _(row):
            push(
                mine.at[STEP[name]], xb.at[level, k_me], t_z.at[level], s_z.at[level],
                row, (level % 2) * NP + r, True,
            )

    def deliver(level, source, n):
        @pl.loop(0, 2 * NP)
        def _(col):
            push(source, out.at[pl.ds(level, n), k_me], t_out.at[level], s_out, r, col, True)

    @pl.when(team)
    def _():
        wait_bytes(r45, s_rows.at[0])
        before = jnp.sum(r45[...], axis=0)
        wait_bytes(r4, s_rows.at[1])
        x4 = jnp.sum(r4[...], axis=0) + before[0]
        gather("x4", x4)
        take(5, 4)
        u4 = mm_t(x4, uinv[4])
        wait_bytes(r5, s_rows.at[2])
        z5 = jnp.sum(r5[...], axis=0) + before[1]
        gathered("x4")
        z5 = z5 - apply(5, 4, "x4")
        gather("z5", z5)
        to_holders(5, "z5")
        deliver(5, mine.at[pl.ds(STEP["z5"], 1)], 1)
        take(4, 5)
        gathered("z5")
        z4 = u4 - apply(4, 5, "z5")
        gather("z4", z4)
        to_holders(4, "z4")
        deliver(4, mine.at[pl.ds(STEP["z4"], 1)], 1)
        take(3, 4)

    @pl.when(odd)
    def _():
        wait_bytes(xb.at[5], s_z.at[5])
        z = xb[5].reshape(64, 128)
        minus(accb, 3, z, mb[3, 2])
        to_team(lambda k: accb.at[3, k], d3.at[q], t_rows.at[3], s_rows.at[3])
        for row in range(3):
            minus(accb, row, z, mb[row, 2])
        to_team(lambda k: accb.at[pl.ds(0, 3), k], d5.at[q], t_rows.at[4], s_rows.at[4])

    @pl.when(team)
    def _():
        wait_bytes(d3, s_rows.at[3])
        z3 = jnp.sum(d3[...], axis=0)
        gathered("z4")
        z3 = z3 - apply(3, 4, "z4")
        gather("z3", z3)
        deliver(3, mine.at[pl.ds(STEP["z3"], 1)], 1)

    @pl.when(even)
    def _():
        wait_bytes(xb.at[4], s_z.at[4])
        z = xb[4].reshape(64, 128)
        for row in range(3):
            minus(accb, row, z, mb[row, 2])
        to_team(lambda k: accb.at[pl.ds(0, 3), k], d4.at[q], t_rows.at[5], s_rows.at[5])

    @pl.when(team)
    def _():
        take(2, 3)
        take(1, 3)
        take(1, 2)
        wait_bytes(d5, s_rows.at[4])
        late = jnp.sum(d5[...], axis=0)
        gathered("z3")
        late2 = late[2] - apply(2, 3, "z3")
        late1 = late[1] - apply(1, 3, "z3")
        wait_bytes(d4, s_rows.at[5])
        last = jnp.sum(d4[...], axis=0)
        gather("z2", late2 + last[2])
        deliver(2, mine.at[pl.ds(STEP["z2"], 1)], 1)
        take(0, 3)
        take(0, 2)
        take(0, 1)
        late0 = late[0] + last[0] - apply(0, 3, "z3")
        gathered("z2")
        gather("z1", late1 + last[1] - apply(1, 2, "z2"))
        late0 = late0 - apply(0, 2, "z2")
        gathered("z1")
        mine[6] = late0 - apply(0, 1, "z1")
        mine[7] = mine[5]
        deliver(0, mine.at[pl.ds(6, 2)], 2)

    @pl.when(jnp.logical_and(diag, even))
    def _():
        @pl.loop(1, NP)
        def _(d):
            wait_bytes(xf.at[0], t_x0.at[d])

    def slices(n):
        return ca.at[pl.ds(0, n)]

    for level in range(3):
        row = level + 1

        @pl.when(jnp.logical_and(par == level % 2, same(row)))
        def _(row=row):
            wait_bytes(slices(NS), t_a.at[row])

        @pl.when(jnp.logical_and(par == row % 2, owner))
        def _(row=row):
            wait_bytes(slices(NP - 1), t_ag.at[row])

        if level + 2 < 4:
            @pl.when(jnp.logical_and(par == level % 2, same(level + 2)))
            def _(row=level + 2):
                @pl.when(diag)
                def _():
                    wait_bytes(slices(NS - 1), t_b.at[row])

                @pl.when(jnp.logical_not(diag))
                def _():
                    wait_bytes(slices(NS), t_b.at[row])

    def sent_rows(i, n):
        @pl.when(team)
        def _():
            wait_bytes(slices((NS - 1) * n), t_rows.at[i])

        @pl.when(jnp.logical_not(team))
        def _():
            wait_bytes(slices(NS * n), t_rows.at[i])

    def sent_blocks(row, col):
        @pl.when(same(col))
        def _():
            i = GROUP[row, col]

            @pl.when(team)
            def _():
                wait_bytes(held.at[pl.ds(0, NS - 1)], t_held.at[i])

            @pl.when(jnp.logical_not(team))
            def _():
                wait_bytes(held.at[pl.ds(0, NS)], t_held.at[i])

    @pl.when(even)
    def _():
        sent_rows(0, 2)
        sent_rows(5, 3)
        for key in ((5, 4), (3, 4), (1, 2), (0, 2)):
            sent_blocks(*key)

    @pl.when(odd)
    def _():
        sent_rows(1, 1)
        sent_rows(2, 1)
        sent_rows(3, 1)
        sent_rows(4, 3)
        for key in ((4, 5), (2, 3), (1, 3), (0, 3), (0, 1)):
            sent_blocks(*key)

    @pl.when(team)
    def _():
        for name, (_, n) in GATHERED.items():
            wait_bytes(slices(n - 1), t_seen.at[STEP[name]])
        for level in (5, 4):
            own_seat = jnp.logical_and(diag, par == level % 2)

            @pl.when(own_seat)
            def _(level=level):
                wait_bytes(slices(NP - 1), t_z.at[level])

            @pl.when(jnp.logical_not(own_seat))
            def _(level=level):
                wait_bytes(slices(NP), t_z.at[level])
        for level in (5, 4, 3, 2):
            wait_bytes(slices(2 * NP - 1), t_out.at[level])
        wait_bytes(slices(2 * (2 * NP - 1)), t_out.at[0])

    wait_bytes(out, s_out)


def shards(rhs, lower, lower_pattern, lower_inv, upper, upper_pattern, upper_inv):
    v = pltpu.VMEM
    dma = pltpu.SemaphoreType.DMA
    slices = (NL, NS, 8, 128)
    parts = (NL * NP, 8, 128)
    blocks = (NL, 3, 128, 128)
    got = pl.pallas_call(
        kernel,
        out_shape=jax.ShapeDtypeStruct(slices, F32),
        in_specs=[pl.BlockSpec(memory_space=pltpu.SMEM)] * 2 + [pl.BlockSpec(memory_space=pl.ANY)] * 5,
        out_specs=pl.BlockSpec(memory_space=pltpu.VMEM),
        scratch_shapes=[
            v((NL, 64, 128), F32), v(blocks, F32), v((NL, 128, 128), F32), v(blocks, F32), v((NL, 128, 128), F32),
            v(blocks, F32), v(blocks, F32), v(slices, F32), v(slices, F32), v(slices, F32), v(slices, F32),
            v(slices, F32), v(parts, F32), v(parts, F32), v((NL, 8, 128), F32),
            v((NHELD, 128, 128), F32), v((NHELD // 2, 128, 256), BF16), v((NHELD // 2, 128, 256), BF16),
            v((NGATHERED, 8, 128), F32), v((8, 8, 128), F32),
            v((NP, 8, 128), F32), v((NP, 8, 128), F32), v((NP, 2, 8, 128), F32),
            v((NP, 8, 128), F32), v((NP, 3, 8, 128), F32), v((NP, 3, 8, 128), F32),
            dma((9,)), dma((NL,)), dma((NL,)), dma((NL,)), dma((NL,)), dma((len(HELD),)), dma((len(GATHERED),)), dma((6,)), dma,
            dma((NP,)), dma((NL,)), dma((NL,)), dma((NL,)), dma((len(HELD),)), dma((len(GATHERED),)), dma((6,)),
            dma((NL,)), dma((NL,)),
        ],
        compiler_params=pltpu.CompilerParams(
            collective_id=0, has_side_effects=True, vmem_limit_bytes=60 * 1024 * 1024
        ),
        name="substitution",
    )(
        lower_pattern.reshape(NL, 3), upper_pattern.reshape(NL, 3), rhs.reshape(NL, 64, 128),
        lower.reshape(blocks), lower_inv.reshape(NL, 128, 128), upper.reshape(blocks), upper_inv.reshape(NL, 128, 128),
    )
    return got.reshape(NL, 1, 64, 128)


def solution(mesh):
    in_specs = (
        P(None, "prow", None, None),
        P(None, "prow", None, "pcol", None, None),
        P(None, "prow", None, "pcol"),
        P(None, "prow", None, None),
        P(None, "prow", None, "pcol", None, None),
        P(None, "prow", None, "pcol"),
        P(None, "prow", None, None),
    )
    out_specs = P(None, "prow", None, None)
    return jax.shard_map(shards, mesh=mesh, in_specs=in_specs, out_specs=out_specs, check_vma=False)
```

time: 1870 us -> 159 us (0.09); the launches traced: 1840 us -> 158 us
  blocking collectives: 1820 us -> 0 us
  Pallas kernels: 0 us -> 154 us
    psum x20 -> x0, blocking collectives: 1820 us -> none  [the longest x10 1110 us: sweep(): total = lax.psum(partial_value, 'pcol')]
    pallas_call x0 -> x1, Pallas kernels: none -> 154 us  [shards(): pl.pallas_call(kernel, out_shape=jax.ShapeDtypeStruct(slices, F32), in_sp...]
where the time goes in v2:
time: 159 us; the launch traced here: 158 us
  Pallas kernels  154 us (97%)
  local copies, waits for them, and re-layouts  4.31 us (3%)
    pallas_call x1, Pallas kernels, shards(): pl.pallas_call(kernel, out_shape=jax.ShapeDtypeStruct(slices, F32), in_sp...  154 us

profile of v2, /device:TPU:1, one launch (start us, length us, event | category | flops | bytes accessed | tf_op | source)
XLA Modules:
  0.0 157.8 jit_solution(11354645536651998514)
XLA Ops:
  0.0 1.4 copy.11
  1.4 1.3 copy.12
  2.7 153.5 %substitution.1 = f32[6,8,8,128]{3,2,1,0:T(8,128)} custom-call(s32[6,3]{1,0:T(8,128)} %bitcast.16, s32[6,3]{1,0:T(8,128)} %bitcast.17, f32[6,64,128]{2,1,0:T(8,128)} %bitcast.15, f32[6,3,128,128]{3,2,1,0:T(8,128)} %bitcast.10, f32[6,128,128]{2,1,0:T(8,128)} %bitcast.13, f32[6,3,128,128]{3,2,1,0:T(8,128)} %bitcast.11, f32[6,128,128]{2,1,0:T(8,128)} %bitcast.14), custom_call_target="tpu_custom_call" | custom-call | tf_op jit(solution)/shard_map/substitution/pallas_call | solution.py:517
  156.2 1.6 %copy.14 = f32[6,1,64,128]{3,2,1,0:T(8,128)} copy(f32[6,1,64,128]{3,2,1,0:T(8,128)} %bitcast.12) | data formatting | bytes 393216

commit v3 on v2

--- a/solution.py
+++ b/solution.py
@@ -11,6 +11,8 @@
 NL = 6
 NP = 16
 NS = 8
+NT = 4
+TR = 16
 BF16 = jnp.bfloat16
 F32 = jnp.float32
 
@@ -67,13 +69,15 @@
     owner = dy < 4
     slot = jnp.where(owner, dy * 2 + lax.rem(r, 2), 0)
     diag = r == q
+
+    def seat(k, row):
+        return 8 * (2 * lax.rem(k, 2) + lax.rem(row, 2)) + 4 * (k // 2) + 2 * lax.rem(k, 2)
+
     col_x, col_z = c // 8, lax.rem(c, 8)
-    turned = lax.rem(col_z + 8 - 2 * lax.rem(col_x, 2), 8)
-    team = lax.rem(turned, 4) == 0
-    k_me = jnp.where(team, col_x * 2 + turned // 4, 0)
-
-    def seat(k):
-        return 8 * (k // 2) + 4 * lax.rem(k, 2) + 2 * lax.rem(k // 2, 2)
+    half = col_x // 2
+    turned = lax.rem(col_z + 8 - 2 * half, 8)
+    team = jnp.logical_and(lax.rem(col_x, 2) == lax.rem(r, 2), lax.rem(turned, 4) == 0)
+    k_me = jnp.where(team, half + 2 * (turned // 4), 0)
 
     def same(level):
         return r // width(level) == q // width(level)
@@ -94,8 +98,11 @@
     @pl.loop(0, NS)
     def _(j):
         tell(near(q, j), c)
-        tell(r, seat(j))
-        tell(q, seat(j))
+
+    @pl.loop(0, NT)
+    def _(k):
+        tell(r, seat(k, r))
+        tell(q, seat(k, q))
 
     @pl.when(owner)
     def _():
@@ -111,7 +118,7 @@
 
         @pl.loop(0, NP)
         def _(k):
-            tell(k, c)
+            tell(k, seat(k_me, k))
 
     loads = [(rhs_h, rhs), (linv_h, linv), (uinv_h, uinv)]
     for m in range(3):
@@ -149,7 +156,7 @@
 
     one = jnp.where(diag, 1, 0)
     sat = jnp.where(team, 1, 0)
-    expected = 2 * NS - one + jnp.where(owner, NP - 1, 0) + NS - sat
+    expected = 2 * NS - one + jnp.where(owner, NP - 1, 0) + NT - sat
     expected = expected + jnp.where(team, 2 * NP - 1 + NP - 1 + 2 * NP - one, 0)
     pl.semaphore_wait(barrier, expected)
 
@@ -183,8 +190,8 @@
             push(source.at[j], target.at[place], send_sem, recv_sem, near(r, j), parity * NP + r, parity is par)
 
     def to_team(piece, target, send_sem, recv_sem):
-        for k in range(NS):
-            push(piece(k), target, send_sem, recv_sem, r, seat(k), True)
+        for k in range(NT):
+            push(piece(pl.ds(2 * k, 2)), target, send_sem, recv_sem, r, seat(k, r), True)
 
     def wait_slices(ref, sem):
         @pl.when(owner)
@@ -201,9 +208,9 @@
 
         @pl.when(same(col))
         def _():
-            @pl.loop(0, NS)
+            @pl.loop(0, NT)
             def _(k):
-                push(source, held.at[first + lax.rem(q, n)], t_held.at[i], s_held.at[i], r, seat(k), True)
+                push(source, held.at[first + lax.rem(q, n)], t_held.at[i], s_held.at[i], r, seat(k, r), True)
 
     def minus(ref, row, x, w):
         ref[row] = ref[row] - mm_t(x, w).reshape(NS, 8, 128)
@@ -306,23 +313,26 @@
     def apply(row, col, name):
         first, n = HELD[row, col]
         base, _ = GATHERED[name]
-        total = jnp.zeros((8, 128), F32)
+        total = jnp.zeros((TR, 128), F32)
         for i in range(n // 2):
-            high, low_ = split(jnp.concatenate([seen[base + 2 * i], seen[base + 2 * i + 1]], axis=1))
+            high, low_ = split(jnp.concatenate(
+                [seen[base + 2 * i].reshape(TR, 128), seen[base + 2 * i + 1].reshape(TR, 128)], axis=1
+            ))
             both = dot_t(jnp.concatenate([high, low_], axis=0), wh[first // 2 + i])
-            total = total + both[0:8] + both[8:16] + dot_t(high, wl[first // 2 + i])
+            total = total + both[0:TR] + both[TR:2 * TR] + dot_t(high, wl[first // 2 + i])
         return total
 
     def gather(name, value):
         base, n = GATHERED[name]
         i = STEP[name]
-        mine[i] = value
+        mine[i] = value.reshape(2, 8, 128)
         place = base + lax.rem(r, n)
-        seen[place] = value
+        seen[place] = value.reshape(2, 8, 128)
 
         @pl.loop(1, n)
         def _(d):
-            push(mine.at[i], seen.at[place], t_seen.at[i], s_seen.at[i], jnp.bitwise_xor(r, d), c, False)
+            row = jnp.bitwise_xor(r, d)
+            push(mine.at[i], seen.at[place], t_seen.at[i], s_seen.at[i], row, seat(k_me, row), False)
 
     def gathered(name):
         base, n = GATHERED[name]
@@ -332,26 +342,26 @@
         @pl.loop(0, NP)
         def _(row):
             push(
-                mine.at[STEP[name]], xb.at[level, k_me], t_z.at[level], s_z.at[level],
+                mine.at[STEP[name]], xb.at[level, pl.ds(2 * k_me, 2)], t_z.at[level], s_z.at[level],
                 row, (level % 2) * NP + r, True,
             )
 
     def deliver(level, source, n):
         @pl.loop(0, 2 * NP)
         def _(col):
-            push(source, out.at[pl.ds(level, n), k_me], t_out.at[level], s_out, r, col, True)
+            push(source, out.at[pl.ds(level, n), pl.ds(2 * k_me, 2)], t_out.at[level], s_out, r, col, True)
 
     @pl.when(team)
     def _():
         wait_bytes(r45, s_rows.at[0])
-        before = jnp.sum(r45[...], axis=0)
+        before = jnp.sum(r45[...], axis=0).reshape(2, TR, 128)
         wait_bytes(r4, s_rows.at[1])
-        x4 = jnp.sum(r4[...], axis=0) + before[0]
+        x4 = jnp.sum(r4[...], axis=0).reshape(TR, 128) + before[0]
         gather("x4", x4)
         take(5, 4)
         u4 = mm_t(x4, uinv[4])
         wait_bytes(r5, s_rows.at[2])
-        z5 = jnp.sum(r5[...], axis=0) + before[1]
+        z5 = jnp.sum(r5[...], axis=0).reshape(TR, 128) + before[1]
         gathered("x4")
         z5 = z5 - apply(5, 4, "x4")
         gather("z5", z5)
@@ -378,7 +388,7 @@
     @pl.when(team)
     def _():
         wait_bytes(d3, s_rows.at[3])
-        z3 = jnp.sum(d3[...], axis=0)
+        z3 = jnp.sum(d3[...], axis=0).reshape(TR, 128)
         gathered("z4")
         z3 = z3 - apply(3, 4, "z4")
         gather("z3", z3)
@@ -398,12 +408,12 @@
         take(1, 3)
         take(1, 2)
         wait_bytes(d5, s_rows.at[4])
-        late = jnp.sum(d5[...], axis=0)
+        late = jnp.sum(d5[...], axis=0).reshape(3, TR, 128)
         gathered("z3")
         late2 = late[2] - apply(2, 3, "z3")
         late1 = late[1] - apply(1, 3, "z3")
         wait_bytes(d4, s_rows.at[5])
-        last = jnp.sum(d4[...], axis=0)
+        last = jnp.sum(d4[...], axis=0).reshape(3, TR, 128)
         gather("z2", late2 + last[2])
         deliver(2, mine.at[pl.ds(STEP["z2"], 1)], 1)
         take(0, 3)
@@ -414,7 +424,7 @@
         gather("z1", late1 + last[1] - apply(1, 2, "z2"))
         late0 = late0 - apply(0, 2, "z2")
         gathered("z1")
-        mine[6] = late0 - apply(0, 1, "z1")
+        mine[6] = (late0 - apply(0, 1, "z1")).reshape(2, 8, 128)
         mine[7] = mine[5]
         deliver(0, mine.at[pl.ds(6, 2)], 2)
 
@@ -452,11 +462,11 @@
     def sent_rows(i, n):
         @pl.when(team)
         def _():
-            wait_bytes(slices((NS - 1) * n), t_rows.at[i])
+            wait_bytes(slices(2 * (NT - 1) * n), t_rows.at[i])
 
         @pl.when(jnp.logical_not(team))
         def _():
-            wait_bytes(slices(NS * n), t_rows.at[i])
+            wait_bytes(slices(2 * NT * n), t_rows.at[i])
 
     def sent_blocks(row, col):
         @pl.when(same(col))
@@ -465,11 +475,11 @@
 
             @pl.when(team)
             def _():
-                wait_bytes(held.at[pl.ds(0, NS - 1)], t_held.at[i])
+                wait_bytes(held.at[pl.ds(0, NT - 1)], t_held.at[i])
 
             @pl.when(jnp.logical_not(team))
             def _():
-                wait_bytes(held.at[pl.ds(0, NS)], t_held.at[i])
+                wait_bytes(held.at[pl.ds(0, NT)], t_held.at[i])
 
     @pl.when(even)
     def _():
@@ -490,20 +500,20 @@
     @pl.when(team)
     def _():
         for name, (_, n) in GATHERED.items():
-            wait_bytes(slices(n - 1), t_seen.at[STEP[name]])
+            wait_bytes(slices(2 * (n - 1)), t_seen.at[STEP[name]])
         for level in (5, 4):
             own_seat = jnp.logical_and(diag, par == level % 2)
 
             @pl.when(own_seat)
             def _(level=level):
-                wait_bytes(slices(NP - 1), t_z.at[level])
+                wait_bytes(slices(2 * (NP - 1)), t_z.at[level])
 
             @pl.when(jnp.logical_not(own_seat))
             def _(level=level):
-                wait_bytes(slices(NP), t_z.at[level])
+                wait_bytes(slices(2 * NP), t_z.at[level])
         for level in (5, 4, 3, 2):
-            wait_bytes(slices(2 * NP - 1), t_out.at[level])
-        wait_bytes(slices(2 * (2 * NP - 1)), t_out.at[0])
+            wait_bytes(slices(2 * (2 * NP - 1)), t_out.at[level])
+        wait_bytes(seen, t_out.at[0])
 
     wait_bytes(out, s_out)
 
@@ -524,9 +534,9 @@
             v(blocks, F32), v(blocks, F32), v(slices, F32), v(slices, F32), v(slices, F32), v(slices, F32),
             v(slices, F32), v(parts, F32), v(parts, F32), v((NL, 8, 128), F32),
             v((NHELD, 128, 128), F32), v((NHELD // 2, 128, 256), BF16), v((NHELD // 2, 128, 256), BF16),
-            v((NGATHERED, 8, 128), F32), v((8, 8, 128), F32),
-            v((NP, 8, 128), F32), v((NP, 8, 128), F32), v((NP, 2, 8, 128), F32),
-            v((NP, 8, 128), F32), v((NP, 3, 8, 128), F32), v((NP, 3, 8, 128), F32),
+            v((NGATHERED, 2, 8, 128), F32), v((8, 2, 8, 128), F32),
+            v((NP, 2, 8, 128), F32), v((NP, 2, 8, 128), F32), v((NP, 2, 2, 8, 128), F32),
+            v((NP, 2, 8, 128), F32), v((NP, 3, 2, 8, 128), F32), v((NP, 3, 2, 8, 128), F32),
             dma((9,)), dma((NL,)), dma((NL,)), dma((NL,)), dma((NL,)), dma((len(HELD),)), dma((len(GATHERED),)), dma((6,)), dma,
             dma((NP,)), dma((NL,)), dma((NL,)), dma((NL,)), dma((len(HELD),)), dma((len(GATHERED),)), dma((6,)),
             dma((NL,)), dma((NL,)),

time: 159 us -> 121 us (0.76)
  Pallas kernels: 154 us -> 115 us
    pallas_call x1, Pallas kernels: 154 us -> 115 us  [shards(): pl.pallas_call(kernel, out_shape=jax.ShapeDtypeStruct(slices, F32), in_sp...]
where the time goes in v3:
time: 121 us; the launch traced here: 119 us
  Pallas kernels  115 us (95%)
  local copies, waits for them, and re-layouts  4.31 us (4%)
    pallas_call x1, Pallas kernels, shards(): pl.pallas_call(kernel, out_shape=jax.ShapeDtypeStruct(slices, F32), in_sp...  115 us

profile of v3, /device:TPU:1, one launch (start us, length us, event | category | flops | bytes accessed | tf_op | source)
XLA Modules:
  0.0 119.0 jit_solution(17522365871347266333)
XLA Ops:
  0.0 1.4 %copy.11 = s32[6,1,3,1]{2,0,3,1:T(8,128)} copy(s32[6,1,3,1]{0,3,2,1:T(1,128)} %param.9) | data formatting | bytes 144 | tf_op jit(solution)/shard_map/reshape | solution.py:549
  1.4 1.3 %copy.12 = s32[6,1,3,1]{2,0,3,1:T(8,128)} copy(s32[6,1,3,1]{0,3,2,1:T(1,128)} %param.12) | data formatting | bytes 144 | tf_op jit(solution)/shard_map/reshape | solution.py:549
  2.7 114.7 %substitution.1 = f32[6,8,8,128]{3,2,1,0:T(8,128)} custom-call(s32[6,3]{1,0:T(8,128)} %bitcast.16, s32[6,3]{1,0:T(8,128)} %bitcast.17, f32[6,64,128]{2,1,0:T(8,128)} %bitcast.15, f32[6,3,128,128]{3,2,1,0:T(8,128)} %bitcast.10, f32[6,128,128]{2,1,0:T(8,128)} %bitcast.13, f32[6,3,128,128]{3,2,1,0:T(8,128)} %bitcast.11, f32[6,128,128]{2,1,0:T(8,128)} %bitcast.14), custom_call_target="tpu_custom_call" | custom-call | tf_op jit(solution)/shard_map/substitution/pallas_call | solution.py:527
  117.4 1.6 %copy.14 = f32[6,1,64,128]{3,2,1,0:T(8,128)} copy(f32[6,1,64,128]{3,2,1,0:T(8,128)} %bitcast.12) | data formatting | bytes 393216

commit v4 on v3

--- a/solution.py
+++ b/solution.py
@@ -57,8 +57,8 @@
 def kernel(
     lpat, upat, rhs_h, low_h, linv_h, upp_h, uinv_h, out,
     rhs, low, linv, upp, uinv, mf, mb, accf, accb, xf, xb, pf, ca, cb, own,
-    held, wh, wl, seen, mine, r4, r5, r45, d3, d5, d4,
-    s_in, s_x, s_z, s_ca, s_cb, s_held, s_seen, s_rows, s_out,
+    e1, held, wh, wl, seen, mine, r4, r5, r45, d3, d5, d4,
+    s_in, s_x, s_z, s_ca, s_cb, s_held, s_seen, s_rows, s_out, s_e1, t_e1,
     t_x0, t_a, t_b, t_ag, t_held, t_seen, t_rows, t_z, t_out,
 ):
     r = lax.axis_index("prow")
@@ -141,7 +141,7 @@
 
     for m in range(3):
         for row in range(2 * m + 1, NL):
-            mf[row, m] = fold(top if row == 5 else linv[row], low[row, m], lpat[row, m])
+            mf[row, m] = fold(top if row == 5 else linv[row], low[row, m], lpat[m, 0, row])
 
     @pl.when(diag)
     def _():
@@ -186,7 +186,7 @@
             push(xf.at[0], xf.at[0], t_x0.at[d], s_x.at[0], jnp.bitwise_xor(r, d), c, False)
 
     def to_owners(source, target, place, send_sem, recv_sem, parity):
-        for j in range(NS):
+        for j in (6, 7, 0, 1, 4, 5, 2, 3):
             push(source.at[j], target.at[place], send_sem, recv_sem, near(r, j), parity * NP + r, parity is par)
 
     def to_team(piece, target, send_sem, recv_sem):
@@ -221,6 +221,15 @@
             @pl.when(jnp.logical_not(diag))
             def _():
                 wait_bytes(xf.at[0], s_x.at[0])
+        elif level == 1:
+            @pl.when(same(2))
+            def _():
+                wait_bytes(e1, s_e1)
+                xf[1] = e1[0] + e1[1]
+
+            @pl.when(jnp.logical_not(same(2)))
+            def _():
+                wait_slices(xf.at[level], s_x.at[level])
         else:
             wait_slices(xf.at[level], s_x.at[level])
         x = xf[level].reshape(64, 128)
@@ -229,6 +238,12 @@
             def _():
                 row = level + 1
                 pf[level] = accf[row] - mm_t(x, mf[row, m]).reshape(NS, 8, 128)
+                if level == 0:
+                    for d in range(4):
+                        push(
+                            pf.at[0], e1.at[lax.rem(q, 2)], t_e1, s_e1,
+                            jnp.bitwise_xor(r, d), NP + r, False,
+                        )
                 to_owners(pf.at[level], ca, row * NP + lax.rem(q, width(row)), t_a.at[row], s_ca.at[row], 1 - par)
 
             row = level + 2
@@ -265,18 +280,32 @@
             wait_bytes(cb.at[pl.ds(level * NP, n)], s_cb.at[level])
             total = total + jnp.sum(cb[level * NP:level * NP + n], axis=0)
         own[level] = total
-        xf[level, slot] = total
-
-        @pl.loop(1, NP)
-        def _(d):
-            push(own.at[level], xf.at[level, slot], t_ag.at[level], s_x.at[level], jnp.bitwise_xor(r, d), c, False)
+        if level > 1:
+            xf[level, slot] = total
+
+            @pl.loop(1, NP)
+            def _(d):
+                row = jnp.bitwise_xor(r, NP - d)
+                push(own.at[level], xf.at[level, slot], t_ag.at[level], s_x.at[level], row, c, False)
+        else:
+            @pl.when(jnp.logical_not(same(2)))
+            def _():
+                xf[level, slot] = total
+
+            @pl.loop(0, NP)
+            def _(d):
+                row = jnp.bitwise_xor(r, d)
+
+                @pl.when(jnp.logical_and(row // 4 != q // 4, row != r))
+                def _():
+                    push(own.at[level], xf.at[level, slot], t_ag.at[level], s_x.at[level], row, c, False)
 
     def prepare_back():
         for copy in copies[6:]:
             copy.wait()
         for m in range(3):
             for row in range(0, 2 * m + 1):
-                mb[row, m] = fold(uinv[row], upp[row, m], upat[row, m])
+                mb[row, m] = fold(uinv[row], upp[row, m], upat[m, 0, row])
 
     @pl.when(even)
     def _():
@@ -292,13 +321,14 @@
     @pl.when(odd)
     def _():
         prepare_back()
-        pl.when(owner)(functools.partial(forward_own, 1))
+        give(4, 5, mb.at[4, 2])
+        pl.when(jnp.logical_and(owner, jnp.logical_not(same(2))))(functools.partial(forward_own, 1))
         forward_hold(1)
-        give(4, 5, mb.at[4, 2])
+        pl.when(jnp.logical_and(owner, same(2)))(functools.partial(forward_own, 1))
+        give(2, 3, mb.at[2, 1])
+        give(1, 3, mb.at[1, 1])
         pl.when(owner)(functools.partial(forward_own, 3))
         forward_hold(3)
-        give(2, 3, mb.at[2, 1])
-        give(1, 3, mb.at[1, 1])
         give(0, 3, mb.at[0, 1])
         give(0, 1, mb.at[0, 0])
 
@@ -331,7 +361,7 @@
 
         @pl.loop(1, n)
         def _(d):
-            row = jnp.bitwise_xor(r, d)
+            row = jnp.bitwise_xor(r, n - d)
             push(mine.at[i], seen.at[place], t_seen.at[i], s_seen.at[i], row, seat(k_me, row), False)
 
     def gathered(name):
@@ -340,7 +370,8 @@
 
     def to_holders(level, name):
         @pl.loop(0, NP)
-        def _(row):
+        def _(d):
+            row = jnp.bitwise_xor(r, NP - 1 - d)
             push(
                 mine.at[STEP[name]], xb.at[level, pl.ds(2 * k_me, 2)], t_z.at[level], s_z.at[level],
                 row, (level % 2) * NP + r, True,
@@ -423,10 +454,10 @@
         gathered("z2")
         gather("z1", late1 + last[1] - apply(1, 2, "z2"))
         late0 = late0 - apply(0, 2, "z2")
+        deliver(1, mine.at[pl.ds(STEP["z1"], 1)], 1)
         gathered("z1")
         mine[6] = (late0 - apply(0, 1, "z1")).reshape(2, 8, 128)
-        mine[7] = mine[5]
-        deliver(0, mine.at[pl.ds(6, 2)], 2)
+        deliver(0, mine.at[pl.ds(6, 1)], 1)
 
     @pl.when(jnp.logical_and(diag, even))
     def _():
@@ -443,10 +474,22 @@
         @pl.when(jnp.logical_and(par == level % 2, same(row)))
         def _(row=row):
             wait_bytes(slices(NS), t_a.at[row])
+            if row == 1:
+                wait_bytes(xf.at[pl.ds(0, 4)], t_e1)
 
         @pl.when(jnp.logical_and(par == row % 2, owner))
         def _(row=row):
-            wait_bytes(slices(NP - 1), t_ag.at[row])
+            if row > 1:
+                wait_bytes(slices(NP - 1), t_ag.at[row])
+                return
+
+            @pl.when(same(2))
+            def _():
+                wait_bytes(slices(NP - 4), t_ag.at[row])
+
+            @pl.when(jnp.logical_not(same(2)))
+            def _():
+                wait_bytes(slices(NP - 5), t_ag.at[row])
 
         if level + 2 < 4:
             @pl.when(jnp.logical_and(par == level % 2, same(level + 2)))
@@ -511,9 +554,8 @@
             @pl.when(jnp.logical_not(own_seat))
             def _(level=level):
                 wait_bytes(slices(2 * NP), t_z.at[level])
-        for level in (5, 4, 3, 2):
+        for level in range(NL):
             wait_bytes(slices(2 * (2 * NP - 1)), t_out.at[level])
-        wait_bytes(seen, t_out.at[0])
 
     wait_bytes(out, s_out)
 
@@ -533,11 +575,11 @@
             v((NL, 64, 128), F32), v(blocks, F32), v((NL, 128, 128), F32), v(blocks, F32), v((NL, 128, 128), F32),
             v(blocks, F32), v(blocks, F32), v(slices, F32), v(slices, F32), v(slices, F32), v(slices, F32),
             v(slices, F32), v(parts, F32), v(parts, F32), v((NL, 8, 128), F32),
-            v((NHELD, 128, 128), F32), v((NHELD // 2, 128, 256), BF16), v((NHELD // 2, 128, 256), BF16),
-            v((NGATHERED, 2, 8, 128), F32), v((8, 2, 8, 128), F32),
+            v((2, NS, 8, 128), F32), v((NHELD, 128, 128), F32), v((NHELD // 2, 128, 256), BF16), v((NHELD // 2, 128, 256), BF16),
+            v((NGATHERED, 2, 8, 128), F32), v((7, 2, 8, 128), F32),
             v((NP, 2, 8, 128), F32), v((NP, 2, 8, 128), F32), v((NP, 2, 2, 8, 128), F32),
             v((NP, 2, 8, 128), F32), v((NP, 3, 2, 8, 128), F32), v((NP, 3, 2, 8, 128), F32),
-            dma((9,)), dma((NL,)), dma((NL,)), dma((NL,)), dma((NL,)), dma((len(HELD),)), dma((len(GATHERED),)), dma((6,)), dma,
+            dma((9,)), dma((NL,)), dma((NL,)), dma((NL,)), dma((NL,)), dma((len(HELD),)), dma((len(GATHERED),)), dma((6,)), dma, dma, dma,
             dma((NP,)), dma((NL,)), dma((NL,)), dma((NL,)), dma((len(HELD),)), dma((len(GATHERED),)), dma((6,)),
             dma((NL,)), dma((NL,)),
         ],
@@ -546,7 +588,7 @@
         ),
         name="substitution",
     )(
-        lower_pattern.reshape(NL, 3), upper_pattern.reshape(NL, 3), rhs.reshape(NL, 64, 128),
+        lower_pattern.transpose(2, 3, 1, 0).reshape(3, 1, NL), upper_pattern.transpose(2, 3, 1, 0).reshape(3, 1, NL), rhs.reshape(NL, 64, 128),
         lower.reshape(blocks), lower_inv.reshape(NL, 128, 128), upper.reshape(blocks), upper_inv.reshape(NL, 128, 128),
     )
     return got.reshape(NL, 1, 64, 128)

time: 121 us -> 104 us (0.86); the launches traced: 119 us -> 104 us
  Pallas kernels: 115 us -> 102 us
  local copies, waits for them, and re-layouts: 4.31 us -> 1.62 us
    pallas_call x1, Pallas kernels: 115 us -> 102 us  [shards(): pl.pallas_call(kernel, out_shape=jax.ShapeDtypeStruct(slices, F32), in_sp...]
    reshape x2 -> x0, local copies, waits for them, and re-layouts: 2.69 us -> none  [the longest x1 1.35 us: shards(): lower_pattern.reshape(NL, 3)]
where the time goes in v4:
time: 104 us
  Pallas kernels  102 us (98%)
  local copies, waits for them, and re-layouts  1.62 us (2%)
    pallas_call x1, Pallas kernels, shards(): pl.pallas_call(kernel, out_shape=jax.ShapeDtypeStruct(slices, F32), in_sp...  102 us

profile of v4, /device:TPU:1, one launch (start us, length us, event | category | flops | bytes accessed | tf_op | source)
XLA Modules:
  0.0 104.0 jit_solution(2125865553986604394)
XLA Ops:
  0.0 102.4 %substitution.1 = f32[6,8,8,128]{3,2,1,0:T(8,128)} custom-call(s32[3,1,6]{2,1,0:T(1,128)} %bitcast.20, s32[3,1,6]{2,1,0:T(1,128)} %bitcast.21, f32[6,64,128]{2,1,0:T(8,128)} %bitcast.19, f32[6,3,128,128]{3,2,1,0:T(8,128)} %bitcast.14, f32[6,128,128]{2,1,0:T(8,128)} %bitcast.17, f32[6,3,128,128]{3,2,1,0:T(8,128)} %bitcast.15, f32[6,128,128]{2,1,0:T(8,128)} %bitcast.18), custom_call_target="tpu_custom_call" | custom-call | tf_op jit(solution)/shard_map/substitution/pallas_call | solution.py:569
  102.4 1.6 %copy.10 = f32[6,1,64,128]{3,2,1,0:T(8,128)} copy(f32[6,1,64,128]{3,2,1,0:T(8,128)} %bitcast.16) | data formatting | bytes 393216

commit v5 on v3

--- a/solution.py
+++ b/solution.py
@@ -57,8 +57,8 @@
 def kernel(
     lpat, upat, rhs_h, low_h, linv_h, upp_h, uinv_h, out,
     rhs, low, linv, upp, uinv, mf, mb, accf, accb, xf, xb, pf, ca, cb, own,
-    held, wh, wl, seen, mine, r4, r5, r45, d3, d5, d4,
-    s_in, s_x, s_z, s_ca, s_cb, s_held, s_seen, s_rows, s_out,
+    e1, m21, held, wh, wl, seen, mine, r4, r5, r45, d3, d5, d4,
+    s_in, s_x, s_z, s_ca, s_cb, s_held, s_seen, s_rows, s_out, s_e1, t_e1, s_m21, t_m21,
     t_x0, t_a, t_b, t_ag, t_held, t_seen, t_rows, t_z, t_out,
 ):
     r = lax.axis_index("prow")
@@ -73,11 +73,16 @@
     def seat(k, row):
         return 8 * (2 * lax.rem(k, 2) + lax.rem(row, 2)) + 4 * (k // 2) + 2 * lax.rem(k, 2)
 
+    def tail_seat(k, row):
+        return seat(k, row) + 1
+
     col_x, col_z = c // 8, lax.rem(c, 8)
     half = col_x // 2
     turned = lax.rem(col_z + 8 - 2 * half, 8)
-    team = jnp.logical_and(lax.rem(col_x, 2) == lax.rem(r, 2), lax.rem(turned, 4) == 0)
-    k_me = jnp.where(team, half + 2 * (turned // 4), 0)
+    seated = lax.rem(col_x, 2) == lax.rem(r, 2)
+    team = jnp.logical_and(seated, lax.rem(turned, 4) == 0)
+    tail = jnp.logical_and(seated, lax.rem(turned, 4) == 1)
+    k_me = jnp.where(jnp.logical_or(team, tail), half + 2 * (turned // 4), 0)
 
     def same(level):
         return r // width(level) == q // width(level)
@@ -102,7 +107,12 @@
     @pl.loop(0, NT)
     def _(k):
         tell(r, seat(k, r))
+        tell(r, tail_seat(k, r))
         tell(q, seat(k, q))
+
+    @pl.when(jnp.logical_and(even, same(2)))
+    def _():
+        tell(r, NP + q)
 
     @pl.when(owner)
     def _():
@@ -110,15 +120,29 @@
         def _(k):
             tell(q, k)
 
-    @pl.when(team)
+    @pl.when(jnp.logical_or(team, tail))
     def _():
         @pl.loop(0, 2 * NP)
         def _(k):
             tell(r, k)
 
+    @pl.when(team)
+    def _():
         @pl.loop(0, NP)
         def _(k):
             tell(k, seat(k_me, k))
+
+    @pl.when(tail)
+    def _():
+        @pl.loop(0, 8)
+        def _(d):
+            row = jnp.bitwise_xor(r, d)
+            tell(row, seat(k_me, row))
+
+        @pl.loop(1, 4)
+        def _(d):
+            row = jnp.bitwise_xor(r, d)
+            tell(row, tail_seat(k_me, row))
 
     loads = [(rhs_h, rhs), (linv_h, linv), (uinv_h, uinv)]
     for m in range(3):
@@ -141,12 +165,12 @@
 
     for m in range(3):
         for row in range(2 * m + 1, NL):
-            mf[row, m] = fold(top if row == 5 else linv[row], low[row, m], lpat[row, m])
+            mf[row, m] = fold(top if row == 5 else linv[row], low[row, m], lpat[m, 0, row])
 
     @pl.when(diag)
     def _():
         for row in range(1, NL):
-            @pl.when(par == (row - 1) % 2)
+            @pl.when(par == (0 if row == 2 else (row - 1) % 2))
             def _(row=row):
                 accf[row] = mm_t(rhs[row], top if row == 5 else linv[row]).reshape(NS, 8, 128)
 
@@ -155,9 +179,11 @@
             xf[0] = mm_t(rhs[0], linv[0]).reshape(NS, 8, 128)
 
     one = jnp.where(diag, 1, 0)
-    sat = jnp.where(team, 1, 0)
-    expected = 2 * NS - one + jnp.where(owner, NP - 1, 0) + NT - sat
-    expected = expected + jnp.where(team, 2 * NP - 1 + NP - 1 + 2 * NP - one, 0)
+    seats = 2 * NT - jnp.where(jnp.logical_or(team, tail), 1, 0)
+    expected = 2 * NS - one + jnp.where(owner, NP - 1, 0) + seats
+    expected = expected + jnp.where(team, 2 * NP - 1 + NP - 1 + 2 * NP - one + 8, 0)
+    expected = expected + jnp.where(tail, 2 * NP - 1 + 3, 0)
+    expected = expected + jnp.where(jnp.logical_and(odd, same(2)), 1, 0)
     pl.semaphore_wait(barrier, expected)
 
     def wait_bytes(ref, sem):
@@ -186,12 +212,12 @@
             push(xf.at[0], xf.at[0], t_x0.at[d], s_x.at[0], jnp.bitwise_xor(r, d), c, False)
 
     def to_owners(source, target, place, send_sem, recv_sem, parity):
-        for j in range(NS):
+        for j in (6, 7, 0, 1, 4, 5, 2, 3):
             push(source.at[j], target.at[place], send_sem, recv_sem, near(r, j), parity * NP + r, parity is par)
 
-    def to_team(piece, target, send_sem, recv_sem):
+    def to_team(piece, target, send_sem, recv_sem, where):
         for k in range(NT):
-            push(piece(pl.ds(2 * k, 2)), target, send_sem, recv_sem, r, seat(k, r), True)
+            push(piece(pl.ds(2 * k, 2)), target, send_sem, recv_sem, r, where(k, r), True)
 
     def wait_slices(ref, sem):
         @pl.when(owner)
@@ -205,12 +231,13 @@
     def give(row, col, source):
         first, n = HELD[row, col]
         i = GROUP[row, col]
+        where = seat if row > 2 else tail_seat
 
         @pl.when(same(col))
         def _():
             @pl.loop(0, NT)
             def _(k):
-                push(source, held.at[first + lax.rem(q, n)], t_held.at[i], s_held.at[i], r, seat(k, r), True)
+                push(source, held.at[first + lax.rem(q, n)], t_held.at[i], s_held.at[i], r, where(k, r), True)
 
     def minus(ref, row, x, w):
         ref[row] = ref[row] - mm_t(x, w).reshape(NS, 8, 128)
@@ -225,18 +252,28 @@
             wait_slices(xf.at[level], s_x.at[level])
         x = xf[level].reshape(64, 128)
         if level < 3:
-            @pl.when(same(level + 1))
-            def _():
-                row = level + 1
-                pf[level] = accf[row] - mm_t(x, mf[row, m]).reshape(NS, 8, 128)
-                to_owners(pf.at[level], ca, row * NP + lax.rem(q, width(row)), t_a.at[row], s_ca.at[row], 1 - par)
+            if level != 1:
+                @pl.when(same(level + 1))
+                def _():
+                    row = level + 1
+                    pf[level] = accf[row] - mm_t(x, mf[row, m]).reshape(NS, 8, 128)
+                    if level == 0:
+                        for d in range(4):
+                            push(
+                                pf.at[0], e1.at[lax.rem(q, 2)], t_e1, s_e1,
+                                jnp.bitwise_xor(r, d), r, True,
+                            )
+                    to_owners(
+                        pf.at[level], ca, row * NP + lax.rem(q, width(row)), t_a.at[row], s_ca.at[row], 1 - par
+                    )
 
             row = level + 2
             if row < 4:
                 @pl.when(same(row))
                 def _():
                     minus(accf, row, x, mf[row, m])
-                    to_owners(accf.at[row], cb, row * NP + lax.rem(q, width(row)), t_b.at[row], s_cb.at[row], par)
+                    if row == 3:
+                        to_owners(accf.at[row], cb, row * NP + lax.rem(q, width(row)), t_b.at[row], s_cb.at[row], par)
 
             for row in range(level + 3, 4):
                 @pl.when(same(row))
@@ -246,22 +283,29 @@
             minus(accf, 4, x, mf[4, m])
             minus(accf, 5, x, mf[5, m])
             if level == 2:
-                to_team(lambda k: accf.at[pl.ds(4, 2), k], r45.at[q], t_rows.at[0], s_rows.at[0])
+                to_team(lambda k: accf.at[pl.ds(4, 2), k], r45.at[q], t_rows.at[0], s_rows.at[0], seat)
         else:
             minus(accf, 4, x, mf[4, m])
-            to_team(lambda k: accf.at[4, k], r4.at[q], t_rows.at[1], s_rows.at[1])
+            to_team(lambda k: accf.at[4, k], r4.at[q], t_rows.at[1], s_rows.at[1], seat)
             minus(accf, 5, x, mf[5, m])
-            to_team(lambda k: accf.at[5, k], r5.at[q], t_rows.at[2], s_rows.at[2])
+            to_team(lambda k: accf.at[5, k], r5.at[q], t_rows.at[2], s_rows.at[2], seat)
 
         @pl.when(diag)
         def _():
             accb[level] = mm_t(x, uinv[level]).reshape(NS, 8, 128)
+
+    def forward_second():
+        wait_bytes(e1, s_e1)
+        x = (e1[0] + e1[1]).reshape(64, 128)
+        wait_bytes(m21, s_m21)
+        pf[1] = accf[2] - mm_t(x, m21[...]).reshape(NS, 8, 128)
+        to_owners(pf.at[1], ca, 2 * NP + lax.rem(q, 4), t_a.at[2], s_ca.at[2], par)
 
     def forward_own(level):
         n = width(level)
         wait_bytes(ca.at[pl.ds(level * NP, n)], s_ca.at[level])
         total = jnp.sum(ca[level * NP:level * NP + n], axis=0)
-        if level >= 2:
+        if level >= 3:
             wait_bytes(cb.at[pl.ds(level * NP, n)], s_cb.at[level])
             total = total + jnp.sum(cb[level * NP:level * NP + n], axis=0)
         own[level] = total
@@ -269,18 +313,20 @@
 
         @pl.loop(1, NP)
         def _(d):
-            push(own.at[level], xf.at[level, slot], t_ag.at[level], s_x.at[level], jnp.bitwise_xor(r, d), c, False)
+            row = jnp.bitwise_xor(r, NP - d)
+            push(own.at[level], xf.at[level, slot], t_ag.at[level], s_x.at[level], row, c, False)
 
     def prepare_back():
         for copy in copies[6:]:
             copy.wait()
         for m in range(3):
             for row in range(0, 2 * m + 1):
-                mb[row, m] = fold(uinv[row], upp[row, m], upat[row, m])
+                mb[row, m] = fold(uinv[row], upp[row, m], upat[m, 0, row])
 
     @pl.when(even)
     def _():
         forward_hold(0)
+        pl.when(same(2))(forward_second)
         give(5, 4, mf.at[5, 2])
         prepare_back()
         pl.when(owner)(functools.partial(forward_own, 2))
@@ -291,14 +337,18 @@
 
     @pl.when(odd)
     def _():
+        @pl.when(same(2))
+        def _():
+            push(mf.at[2, 0], m21, t_m21, s_m21, r, q, False)
+
         prepare_back()
+        give(4, 5, mb.at[4, 2])
         pl.when(owner)(functools.partial(forward_own, 1))
         forward_hold(1)
-        give(4, 5, mb.at[4, 2])
+        give(2, 3, mb.at[2, 1])
+        give(1, 3, mb.at[1, 1])
         pl.when(owner)(functools.partial(forward_own, 3))
         forward_hold(3)
-        give(2, 3, mb.at[2, 1])
-        give(1, 3, mb.at[1, 1])
         give(0, 3, mb.at[0, 1])
         give(0, 1, mb.at[0, 0])
 
@@ -325,22 +375,25 @@
     def gather(name, value):
         base, n = GATHERED[name]
         i = STEP[name]
+        where = seat if n == NP else tail_seat
         mine[i] = value.reshape(2, 8, 128)
         place = base + lax.rem(r, n)
-        seen[place] = value.reshape(2, 8, 128)
-
-        @pl.loop(1, n)
+        if name != "z3":
+            seen[place] = value.reshape(2, 8, 128)
+
+        @pl.loop(0 if name == "z3" else 1, n)
         def _(d):
-            row = jnp.bitwise_xor(r, d)
-            push(mine.at[i], seen.at[place], t_seen.at[i], s_seen.at[i], row, seat(k_me, row), False)
+            row = jnp.bitwise_xor(r, n - 1 - d if name == "z3" else n - d)
+            push(mine.at[i], seen.at[place], t_seen.at[i], s_seen.at[i], row, where(k_me, row), False)
 
     def gathered(name):
         base, n = GATHERED[name]
-        wait_bytes(seen.at[pl.ds(base, n - 1)], s_seen.at[STEP[name]])
+        wait_bytes(seen.at[pl.ds(base, n if name == "z3" else n - 1)], s_seen.at[STEP[name]])
 
     def to_holders(level, name):
         @pl.loop(0, NP)
-        def _(row):
+        def _(d):
+            row = jnp.bitwise_xor(r, NP - 1 - d)
             push(
                 mine.at[STEP[name]], xb.at[level, pl.ds(2 * k_me, 2)], t_z.at[level], s_z.at[level],
                 row, (level % 2) * NP + r, True,
@@ -380,10 +433,10 @@
         wait_bytes(xb.at[5], s_z.at[5])
         z = xb[5].reshape(64, 128)
         minus(accb, 3, z, mb[3, 2])
-        to_team(lambda k: accb.at[3, k], d3.at[q], t_rows.at[3], s_rows.at[3])
+        to_team(lambda k: accb.at[3, k], d3.at[q], t_rows.at[3], s_rows.at[3], seat)
         for row in range(3):
             minus(accb, row, z, mb[row, 2])
-        to_team(lambda k: accb.at[pl.ds(0, 3), k], d5.at[q], t_rows.at[4], s_rows.at[4])
+        to_team(lambda k: accb.at[pl.ds(0, 3), k], d5.at[q], t_rows.at[4], s_rows.at[4], tail_seat)
 
     @pl.when(team)
     def _():
@@ -398,11 +451,13 @@
     def _():
         wait_bytes(xb.at[4], s_z.at[4])
         z = xb[4].reshape(64, 128)
-        for row in range(3):
+        minus(accb, 2, z, mb[2, 2])
+        to_team(lambda k: accb.at[2, k], d4.at[q, 2], t_rows.at[6], s_rows.at[6], tail_seat)
+        for row in range(2):
             minus(accb, row, z, mb[row, 2])
-        to_team(lambda k: accb.at[pl.ds(0, 3), k], d4.at[q], t_rows.at[5], s_rows.at[5])
-
-    @pl.when(team)
+        to_team(lambda k: accb.at[pl.ds(0, 2), k], d4.at[q, pl.ds(0, 2)], t_rows.at[5], s_rows.at[5], tail_seat)
+
+    @pl.when(tail)
     def _():
         take(2, 3)
         take(1, 3)
@@ -412,10 +467,11 @@
         gathered("z3")
         late2 = late[2] - apply(2, 3, "z3")
         late1 = late[1] - apply(1, 3, "z3")
-        wait_bytes(d4, s_rows.at[5])
-        last = jnp.sum(d4[...], axis=0).reshape(3, TR, 128)
-        gather("z2", late2 + last[2])
+        wait_bytes(r4, s_rows.at[6])
+        gather("z2", late2 + jnp.sum(d4[:, 2], axis=0).reshape(TR, 128))
         deliver(2, mine.at[pl.ds(STEP["z2"], 1)], 1)
+        wait_bytes(r45, s_rows.at[5])
+        last = jnp.sum(d4[:, 0:2], axis=0).reshape(2, TR, 128)
         take(0, 3)
         take(0, 2)
         take(0, 1)
@@ -423,10 +479,17 @@
         gathered("z2")
         gather("z1", late1 + last[1] - apply(1, 2, "z2"))
         late0 = late0 - apply(0, 2, "z2")
+        deliver(1, mine.at[pl.ds(STEP["z1"], 1)], 1)
         gathered("z1")
         mine[6] = (late0 - apply(0, 1, "z1")).reshape(2, 8, 128)
-        mine[7] = mine[5]
-        deliver(0, mine.at[pl.ds(6, 2)], 2)
+        for dx in (2, 1, 3, 0):
+            for dz in (4, 3, 5, 2, 6, 1, 7, 0):
+                col = 8 * lax.rem(col_x + dx, 4) + lax.rem(col_z + dz, 8)
+                piece = out.at[pl.ds(0, 1), pl.ds(2 * k_me, 2)]
+                if dx == dz == 0:
+                    pltpu.make_async_copy(mine.at[pl.ds(6, 1)], piece, s_out).start()
+                else:
+                    push(mine.at[pl.ds(6, 1)], piece, t_out.at[0], s_out, r, col, False)
 
     @pl.when(jnp.logical_and(diag, even))
     def _():
@@ -437,34 +500,56 @@
     def slices(n):
         return ca.at[pl.ds(0, n)]
 
-    for level in range(3):
-        row = level + 1
-
-        @pl.when(jnp.logical_and(par == level % 2, same(row)))
-        def _(row=row):
-            wait_bytes(slices(NS), t_a.at[row])
-
+    def sent_slices(sem, n):
+        @pl.when(diag)
+        def _():
+            wait_bytes(slices(n - 1), sem)
+
+        @pl.when(jnp.logical_not(diag))
+        def _():
+            wait_bytes(slices(n), sem)
+
+    @pl.when(jnp.logical_and(even, same(1)))
+    def _():
+        wait_bytes(slices(NS), t_a.at[1])
+
+        @pl.when(diag)
+        def _():
+            wait_bytes(xf.at[pl.ds(0, 3)], t_e1)
+
+        @pl.when(jnp.logical_not(diag))
+        def _():
+            wait_bytes(xf.at[pl.ds(0, 4)], t_e1)
+
+    @pl.when(jnp.logical_and(even, same(2)))
+    def _():
+        sent_slices(t_a.at[2], NS)
+
+    @pl.when(jnp.logical_and(even, same(3)))
+    def _():
+        wait_bytes(slices(NS), t_a.at[3])
+
+    @pl.when(jnp.logical_and(odd, same(2)))
+    def _():
+        wait_bytes(m21, t_m21)
+
+    @pl.when(jnp.logical_and(odd, same(3)))
+    def _():
+        sent_slices(t_b.at[3], NS)
+
+    for row in range(1, 4):
         @pl.when(jnp.logical_and(par == row % 2, owner))
         def _(row=row):
             wait_bytes(slices(NP - 1), t_ag.at[row])
 
-        if level + 2 < 4:
-            @pl.when(jnp.logical_and(par == level % 2, same(level + 2)))
-            def _(row=level + 2):
-                @pl.when(diag)
-                def _():
-                    wait_bytes(slices(NS - 1), t_b.at[row])
-
-                @pl.when(jnp.logical_not(diag))
-                def _():
-                    wait_bytes(slices(NS), t_b.at[row])
-
     def sent_rows(i, n):
-        @pl.when(team)
+        kept = tail if i > 3 else team
+
+        @pl.when(kept)
         def _():
             wait_bytes(slices(2 * (NT - 1) * n), t_rows.at[i])
 
-        @pl.when(jnp.logical_not(team))
+        @pl.when(jnp.logical_not(kept))
         def _():
             wait_bytes(slices(2 * NT * n), t_rows.at[i])
 
@@ -472,19 +557,21 @@
         @pl.when(same(col))
         def _():
             i = GROUP[row, col]
-
-            @pl.when(team)
+            kept = team if row > 2 else tail
+
+            @pl.when(kept)
             def _():
                 wait_bytes(held.at[pl.ds(0, NT - 1)], t_held.at[i])
 
-            @pl.when(jnp.logical_not(team))
+            @pl.when(jnp.logical_not(kept))
             def _():
                 wait_bytes(held.at[pl.ds(0, NT)], t_held.at[i])
 
     @pl.when(even)
     def _():
         sent_rows(0, 2)
-        sent_rows(5, 3)
+        sent_rows(5, 2)
+        sent_rows(6, 1)
         for key in ((5, 4), (3, 4), (1, 2), (0, 2)):
             sent_blocks(*key)
 
@@ -499,8 +586,9 @@
 
     @pl.when(team)
     def _():
-        for name, (_, n) in GATHERED.items():
-            wait_bytes(slices(2 * (n - 1)), t_seen.at[STEP[name]])
+        for name in ("x4", "z5", "z4"):
+            wait_bytes(slices(2 * (NP - 1)), t_seen.at[STEP[name]])
+        wait_bytes(slices(2 * 8), t_seen.at[STEP["z3"]])
         for level in (5, 4):
             own_seat = jnp.logical_and(diag, par == level % 2)
 
@@ -511,9 +599,15 @@
             @pl.when(jnp.logical_not(own_seat))
             def _(level=level):
                 wait_bytes(slices(2 * NP), t_z.at[level])
-        for level in (5, 4, 3, 2):
+        for level in (5, 4, 3):
             wait_bytes(slices(2 * (2 * NP - 1)), t_out.at[level])
-        wait_bytes(seen, t_out.at[0])
+
+    @pl.when(tail)
+    def _():
+        wait_bytes(slices(2 * 3), t_seen.at[STEP["z2"]])
+        wait_bytes(slices(2 * 1), t_seen.at[STEP["z1"]])
+        for level in (2, 1, 0):
+            wait_bytes(slices(2 * (2 * NP - 1)), t_out.at[level])
 
     wait_bytes(out, s_out)
 
@@ -533,12 +627,12 @@
             v((NL, 64, 128), F32), v(blocks, F32), v((NL, 128, 128), F32), v(blocks, F32), v((NL, 128, 128), F32),
             v(blocks, F32), v(blocks, F32), v(slices, F32), v(slices, F32), v(slices, F32), v(slices, F32),
             v(slices, F32), v(parts, F32), v(parts, F32), v((NL, 8, 128), F32),
-            v((NHELD, 128, 128), F32), v((NHELD // 2, 128, 256), BF16), v((NHELD // 2, 128, 256), BF16),
-            v((NGATHERED, 2, 8, 128), F32), v((8, 2, 8, 128), F32),
+            v((2, NS, 8, 128), F32), v((128, 128), F32), v((NHELD, 128, 128), F32), v((NHELD // 2, 128, 256), BF16), v((NHELD // 2, 128, 256), BF16),
+            v((NGATHERED, 2, 8, 128), F32), v((7, 2, 8, 128), F32),
             v((NP, 2, 8, 128), F32), v((NP, 2, 8, 128), F32), v((NP, 2, 2, 8, 128), F32),
             v((NP, 2, 8, 128), F32), v((NP, 3, 2, 8, 128), F32), v((NP, 3, 2, 8, 128), F32),
-            dma((9,)), dma((NL,)), dma((NL,)), dma((NL,)), dma((NL,)), dma((len(HELD),)), dma((len(GATHERED),)), dma((6,)), dma,
-            dma((NP,)), dma((NL,)), dma((NL,)), dma((NL,)), dma((len(HELD),)), dma((len(GATHERED),)), dma((6,)),
+            dma((9,)), dma((NL,)), dma((NL,)), dma((NL,)), dma((NL,)), dma((len(HELD),)), dma((len(GATHERED),)), dma((7,)), dma, dma, dma, dma, dma,
+            dma((NP,)), dma((NL,)), dma((NL,)), dma((NL,)), dma((len(HELD),)), dma((len(GATHERED),)), dma((7,)),
             dma((NL,)), dma((NL,)),
         ],
         compiler_params=pltpu.CompilerParams(
@@ -546,7 +640,7 @@
         ),
         name="substitution",
     )(
-        lower_pattern.reshape(NL, 3), upper_pattern.reshape(NL, 3), rhs.reshape(NL, 64, 128),
+        lower_pattern.transpose(2, 3, 1, 0).reshape(3, 1, NL), upper_pattern.transpose(2, 3, 1, 0).reshape(3, 1, NL), rhs.reshape(NL, 64, 128),
         lower.reshape(blocks), lower_inv.reshape(NL, 128, 128), upper.reshape(blocks), upper_inv.reshape(NL, 128, 128),
     )
     return got.reshape(NL, 1, 64, 128)

time: 121 us -> 102 us (0.84); the launches traced: 119 us -> 101 us
  Pallas kernels: 115 us -> 99.8 us
  local copies, waits for them, and re-layouts: 4.31 us -> 1.62 us
    pallas_call x1, Pallas kernels: 115 us -> 99.8 us  [shards(): pl.pallas_call(kernel, out_shape=jax.ShapeDtypeStruct(slices, F32), in_sp...]
    reshape x2 -> x0, local copies, waits for them, and re-layouts: 2.69 us -> none  [the longest x1 1.35 us: shards(): lower_pattern.reshape(NL, 3)]
where the time goes in v5:
time: 102 us; the launch traced here: 101 us
  Pallas kernels  99.8 us (98%)
  local copies, waits for them, and re-layouts  1.62 us (2%)
    pallas_call x1, Pallas kernels, shards(): pl.pallas_call(kernel, out_shape=jax.ShapeDtypeStruct(slices, F32), in_sp...  99.8 us

profile of v5, /device:TPU:1, one launch (start us, length us, event | category | flops | bytes accessed | tf_op | source)
XLA Modules:
  0.0 101.5 jit_solution(6533964551883860820)
XLA Ops:
  0.0 99.8 %substitution.1 = f32[6,8,8,128]{3,2,1,0:T(8,128)} custom-call(s32[3,1,6]{2,1,0:T(1,128)} %bitcast.20, s32[3,1,6]{2,1,0:T(1,128)} %bitcast.21, f32[6,64,128]{2,1,0:T(8,128)} %bitcast.19, f32[6,3,128,128]{3,2,1,0:T(8,128)} %bitcast.14, f32[6,128,128]{2,1,0:T(8,128)} %bitcast.17, f32[6,3,128,128]{3,2,1,0:T(8,128)} %bitcast.15, f32[6,128,128]{2,1,0:T(8,128)} %bitcast.18), custom_call_target="tpu_custom_call" | custom-call | tf_op jit(solution)/shard_map/substitution/pallas_call | solution.py:621
  99.8 1.6 %copy.10 = f32[6,1,64,128]{3,2,1,0:T(8,128)} copy(f32[6,1,64,128]{3,2,1,0:T(8,128)} %bitcast.16) | data formatting | bytes 393216

commit v6 on v5

--- a/solution.py
+++ b/solution.py
@@ -79,10 +79,10 @@
     col_x, col_z = c // 8, lax.rem(c, 8)
     half = col_x // 2
     turned = lax.rem(col_z + 8 - 2 * half, 8)
-    seated = lax.rem(col_x, 2) == lax.rem(r, 2)
-    team = jnp.logical_and(seated, lax.rem(turned, 4) == 0)
-    tail = jnp.logical_and(seated, lax.rem(turned, 4) == 1)
-    k_me = jnp.where(jnp.logical_or(team, tail), half + 2 * (turned // 4), 0)
+    team = jnp.logical_and(lax.rem(col_x, 2) == lax.rem(r, 2), lax.rem(turned, 4) == 0)
+    k_tail = half + 2 * (turned // 4)
+    tail = c == tail_seat(k_tail, r)
+    k_me = jnp.where(tail, k_tail, jnp.where(team, half + 2 * (turned // 4), 0))
 
     def same(level):
         return r // width(level) == q // width(level)
@@ -100,25 +100,28 @@
         def _():
             pl.semaphore_signal(barrier, inc=1, device_id=at(row, col), device_id_type=MESH)
 
-    @pl.loop(0, NS)
-    def _(j):
-        tell(near(q, j), c)
+    @pl.loop(0, NT)
+    def _(k):
+        tell(q, seat(k, q))
+
+    @pl.when(owner)
+    def _():
+        @pl.loop(0, 2 * NP)
+        def _(k):
+            tell(q, k)
 
     @pl.loop(0, NT)
     def _(k):
         tell(r, seat(k, r))
         tell(r, tail_seat(k, r))
-        tell(q, seat(k, q))
+
+    @pl.loop(0, NS)
+    def _(j):
+        tell(near(q, j), c)
 
     @pl.when(jnp.logical_and(even, same(2)))
     def _():
         tell(r, NP + q)
-
-    @pl.when(owner)
-    def _():
-        @pl.loop(0, 2 * NP)
-        def _(k):
-            tell(q, k)
 
     @pl.when(jnp.logical_or(team, tail))
     def _():
@@ -155,28 +158,32 @@
 
     accf[...] = jnp.zeros_like(accf)
     accb[...] = jnp.zeros_like(accb)
-    for copy in copies[:6]:
-        copy.wait()
-
-    top = mm(uinv[5], linv[5])
-
     def fold(inv, block, bit):
         return mm(inv, block * bit.astype(F32))
 
-    for m in range(3):
-        for row in range(2 * m + 1, NL):
-            mf[row, m] = fold(top if row == 5 else linv[row], low[row, m], lpat[m, 0, row])
-
-    @pl.when(diag)
-    def _():
-        for row in range(1, NL):
-            @pl.when(par == (0 if row == 2 else (row - 1) % 2))
-            def _(row=row):
-                accf[row] = mm_t(rhs[row], top if row == 5 else linv[row]).reshape(NS, 8, 128)
-
-        @pl.when(even)
-        def _():
-            xf[0] = mm_t(rhs[0], linv[0]).reshape(NS, 8, 128)
+    for i in (0, 1, 3):
+        copies[i].wait()
+    for row in (1, 2):
+        mf[row, 0] = fold(linv[row], low[row, 0], lpat[0, 0, row])
+
+    @pl.when(jnp.logical_and(diag, even))
+    def _():
+        for row in (1, 2):
+            accf[row] = mm_t(rhs[row], linv[row]).reshape(NS, 8, 128)
+        xf[0] = mm_t(rhs[0], linv[0]).reshape(NS, 8, 128)
+
+    def prepare_forward():
+        top = mm(uinv[5], linv[5])
+        for m in range(2):
+            for row in range(3, NL):
+                mf[row, m] = fold(top if row == 5 else linv[row], low[row, m], lpat[m, 0, row])
+
+        @pl.when(diag)
+        def _():
+            for row in range(3, NL):
+                @pl.when(par == (row - 1) % 2)
+                def _(row=row):
+                    accf[row] = mm_t(rhs[row], top if row == 5 else linv[row]).reshape(NS, 8, 128)
 
     one = jnp.where(diag, 1, 0)
     seats = 2 * NT - jnp.where(jnp.logical_or(team, tail), 1, 0)
@@ -267,6 +274,8 @@
                         pf.at[level], ca, row * NP + lax.rem(q, width(row)), t_a.at[row], s_ca.at[row], 1 - par
                     )
 
+            if level == 0:
+                prepare_forward()
             row = level + 2
             if row < 4:
                 @pl.when(same(row))
@@ -317,17 +326,27 @@
             push(own.at[level], xf.at[level, slot], t_ag.at[level], s_x.at[level], row, c, False)
 
     def prepare_back():
-        for copy in copies[6:]:
-            copy.wait()
         for m in range(3):
-            for row in range(0, 2 * m + 1):
+            for row in range(0, min(4, 2 * m + 1)):
                 mb[row, m] = fold(uinv[row], upp[row, m], upat[m, 0, row])
 
+    def first_wide():
+        mf[5, 2] = fold(mm(uinv[5], linv[5]), low[5, 2], lpat[2, 0, 5])
+        give(5, 4, mf.at[5, 2])
+
+    for i in (2, 4, 5, 6, 7, 8):
+        copies[i].wait()
+
     @pl.when(even)
     def _():
+        pl.when(jnp.logical_not(same(2)))(first_wide)
         forward_hold(0)
-        pl.when(same(2))(forward_second)
-        give(5, 4, mf.at[5, 2])
+
+        @pl.when(same(2))
+        def _():
+            forward_second()
+            first_wide()
+
         prepare_back()
         pl.when(owner)(functools.partial(forward_own, 2))
         forward_hold(2)
@@ -341,8 +360,10 @@
         def _():
             push(mf.at[2, 0], m21, t_m21, s_m21, r, q, False)
 
+        mb[4, 2] = fold(uinv[4], upp[4, 2], upat[2, 0, 4])
+        give(4, 5, mb.at[4, 2])
+        prepare_forward()
         prepare_back()
-        give(4, 5, mb.at[4, 2])
         pl.when(owner)(functools.partial(forward_own, 1))
         forward_hold(1)
         give(2, 3, mb.at[2, 1])
@@ -403,6 +424,16 @@
         @pl.loop(0, 2 * NP)
         def _(col):
             push(source, out.at[pl.ds(level, n), pl.ds(2 * k_me, 2)], t_out.at[level], s_out, r, col, True)
+
+    def deliver_far_first(level, source):
+        target = out.at[pl.ds(level, 1), pl.ds(2 * k_me, 2)]
+        for dx in (2, 1, 3, 0):
+            for dz in (4, 3, 5, 2, 6, 1, 7, 0):
+                if dx == dz == 0:
+                    pltpu.make_async_copy(source, target, s_out).start()
+                else:
+                    col = 8 * lax.rem(col_x + dx, 4) + lax.rem(col_z + dz, 8)
+                    push(source, target, t_out.at[level], s_out, r, col, False)
 
     @pl.when(team)
     def _():
@@ -467,29 +498,23 @@
         gathered("z3")
         late2 = late[2] - apply(2, 3, "z3")
         late1 = late[1] - apply(1, 3, "z3")
+        take(0, 3)
+        take(0, 2)
+        take(0, 1)
+        late0 = late[0] - apply(0, 3, "z3")
         wait_bytes(r4, s_rows.at[6])
         gather("z2", late2 + jnp.sum(d4[:, 2], axis=0).reshape(TR, 128))
         deliver(2, mine.at[pl.ds(STEP["z2"], 1)], 1)
         wait_bytes(r45, s_rows.at[5])
         last = jnp.sum(d4[:, 0:2], axis=0).reshape(2, TR, 128)
-        take(0, 3)
-        take(0, 2)
-        take(0, 1)
-        late0 = late[0] + last[0] - apply(0, 3, "z3")
+        late0 = late0 + last[0]
         gathered("z2")
         gather("z1", late1 + last[1] - apply(1, 2, "z2"))
         late0 = late0 - apply(0, 2, "z2")
-        deliver(1, mine.at[pl.ds(STEP["z1"], 1)], 1)
+        deliver_far_first(1, mine.at[pl.ds(STEP["z1"], 1)])
         gathered("z1")
         mine[6] = (late0 - apply(0, 1, "z1")).reshape(2, 8, 128)
-        for dx in (2, 1, 3, 0):
-            for dz in (4, 3, 5, 2, 6, 1, 7, 0):
-                col = 8 * lax.rem(col_x + dx, 4) + lax.rem(col_z + dz, 8)
-                piece = out.at[pl.ds(0, 1), pl.ds(2 * k_me, 2)]
-                if dx == dz == 0:
-                    pltpu.make_async_copy(mine.at[pl.ds(6, 1)], piece, s_out).start()
-                else:
-                    push(mine.at[pl.ds(6, 1)], piece, t_out.at[0], s_out, r, col, False)
+        deliver_far_first(0, mine.at[pl.ds(6, 1)])
 
     @pl.when(jnp.logical_and(diag, even))
     def _():

time: 102 us -> 100 us (0.980)
  Pallas kernels: 99.8 us -> 98.3 us
    pallas_call x1, Pallas kernels: 99.8 us -> 98.3 us  [shards(): pl.pallas_call(kernel, out_shape=jax.ShapeDtypeStruct(slices, F32), in_sp...]
where the time goes in v6:
time: 100 us; the launch traced here: 99.9 us
  Pallas kernels  98.3 us (98%)
  local copies, waits for them, and re-layouts  1.62 us (2%)
    pallas_call x1, Pallas kernels, shards(): pl.pallas_call(kernel, out_shape=jax.ShapeDtypeStruct(slices, F32), in_sp...  98.3 us

profile of v6, /device:TPU:1, one launch (start us, length us, event | category | flops | bytes accessed | tf_op | source)
XLA Modules:
  0.0 99.9 jit_solution(14482093880463703848)
XLA Ops:
  0.0 98.3 %substitution.1 = f32[6,8,8,128]{3,2,1,0:T(8,128)} custom-call(s32[3,1,6]{2,1,0:T(1,128)} %bitcast.20, s32[3,1,6]{2,1,0:T(1,128)} %bitcast.21, f32[6,64,128]{2,1,0:T(8,128)} %bitcast.19, f32[6,3,128,128]{3,2,1,0:T(8,128)} %bitcast.14, f32[6,128,128]{2,1,0:T(8,128)} %bitcast.17, f32[6,3,128,128]{3,2,1,0:T(8,128)} %bitcast.15, f32[6,128,128]{2,1,0:T(8,128)} %bitcast.18), custom_call_target="tpu_custom_call" | custom-call | tf_op jit(solution)/shard_map/substitution/pallas_call | solution.py:646
  98.3 1.6 %copy.10 = f32[6,1,64,128]{3,2,1,0:T(8,128)} copy(f32[6,1,64,128]{3,2,1,0:T(8,128)} %bitcast.16) | data formatting | bytes 393216

commit v7 on v6

--- a/solution.py
+++ b/solution.py
@@ -100,10 +100,6 @@
         def _():
             pl.semaphore_signal(barrier, inc=1, device_id=at(row, col), device_id_type=MESH)
 
-    @pl.loop(0, NT)
-    def _(k):
-        tell(q, seat(k, q))
-
     @pl.when(owner)
     def _():
         @pl.loop(0, 2 * NP)
@@ -188,7 +184,7 @@
     one = jnp.where(diag, 1, 0)
     seats = 2 * NT - jnp.where(jnp.logical_or(team, tail), 1, 0)
     expected = 2 * NS - one + jnp.where(owner, NP - 1, 0) + seats
-    expected = expected + jnp.where(team, 2 * NP - 1 + NP - 1 + 2 * NP - one + 8, 0)
+    expected = expected + jnp.where(team, 2 * NP - 1 + NP - 1 + 8, 0)
     expected = expected + jnp.where(tail, 2 * NP - 1 + 3, 0)
     expected = expected + jnp.where(jnp.logical_and(odd, same(2)), 1, 0)
     pl.semaphore_wait(barrier, expected)

time: 100 us -> 100 us (level)
  no operation moved by 1% of the time
where the time goes in v7:
time: 100 us
  Pallas kernels  98.6 us (99%)
  local copies, waits for them, and re-layouts  1.62 us (2%)
    pallas_call x1, Pallas kernels, shards(): pl.pallas_call(kernel, out_shape=jax.ShapeDtypeStruct(slices, F32), in_sp...  98.6 us

profile of v7, /device:TPU:1, one launch (start us, length us, event | category | flops | bytes accessed | tf_op | source)
XLA Modules:
  0.0 100.3 jit_solution(6851023310624696069)
XLA Ops:
  0.0 98.6 %substitution.1 = f32[6,8,8,128]{3,2,1,0:T(8,128)} custom-call(s32[3,1,6]{2,1,0:T(1,128)} %bitcast.20, s32[3,1,6]{2,1,0:T(1,128)} %bitcast.21, f32[6,64,128]{2,1,0:T(8,128)} %bitcast.19, f32[6,3,128,128]{3,2,1,0:T(8,128)} %bitcast.14, f32[6,128,128]{2,1,0:T(8,128)} %bitcast.17, f32[6,3,128,128]{3,2,1,0:T(8,128)} %bitcast.15, f32[6,128,128]{2,1,0:T(8,128)} %bitcast.18), custom_call_target="tpu_custom_call" | custom-call | tf_op jit(solution)/shard_map/substitution/pallas_call | solution.py:642
  98.7 1.6 %copy.10 = f32[6,1,64,128]{3,2,1,0:T(8,128)} copy(f32[6,1,64,128]{3,2,1,0:T(8,128)} %bitcast.16) | data formatting | bytes 393216
